TPU v7x, 256 devices: a whole 4x4x8 slice. The times are simulated.
256 devices in a mesh: dp: 8 (over x, core), pencil: 32 (over y, z).
Axes of the slice: x: 4, y: 4, z: 8, core: 2. Of those that a mesh axis runs over, the one named last changes fastest.
Arguments:
- field: bfloat16 [8, 512, 512, 128], P('dp', 'pencil'), may hold values from -6 to 6
- cotangent: bfloat16 [8, 512, 512, 128], P('dp', 'pencil'), may hold values from -6 to 6
- first_core: float32 [32, 16], replicated, may hold values from -6 to 6
- second_core: float32 [16, 32, 16], P(None, 'pencil'), may hold values from -1.5 to 1.5
- output_core: float32 [16, 32, 16], replicated, may hold values from -1.5 to 1.5
- input_core: float32 [16, 32], replicated, may hold values from -1.5 to 1.5
- channel_mix: bfloat16 [32, 32], replicated, may hold values from -1 to 1
- channel_bias: float32 [32], replicated, may hold values from -3 to 3
Outputs:
- activated: bfloat16 [8, 512, 512, 128], P('dp', 'pencil')
- field_adjoint: bfloat16 [8, 512, 512, 128], P('dp', 'pencil')
- first_adjoint: float32 [32, 16], replicated
- second_adjoint: float32 [16, 32, 16], P(None, 'pencil')
- output_adjoint: float32 [16, 32, 16], replicated
- input_adjoint: float32 [16, 32], replicated
- mix_adjoint: float32 [32, 32], replicated
- bias_adjoint: float32 [32], replicated
All inputs are finite; a program needn't handle non-finite values.
Results may differ from a plain program's by a relative error of at most 0.034.
Values may be sent and summed in bfloat16 or wider, within the bound.
A program may use at most 64 MiB of HBM per device.

v0:
```python
import math

import jax
import jax.numpy as jnp
from jax import lax
from jax.sharding import PartitionSpec as P

PRECISE = lax.Precision.HIGHEST


def build_second(points, retained, length):
    positions = jnp.arange(length, dtype=jnp.int32)
    frequency = jnp.arange(retained, dtype=jnp.int32)
    phases = positions[:, None] * frequency[None, :] % points
    angles = phases.astype(jnp.float32) * (2.0 * math.pi / points)
    factor = 1.0 / math.sqrt(points)
    stacked = jnp.stack([jnp.cos(angles) * factor, -jnp.sin(angles) * factor], axis=2)
    return stacked.reshape(length, 2 * retained).astype(jnp.bfloat16)


def build_first(points, retained, offset, length):
    positions = jnp.arange(length, dtype=jnp.int32) + offset
    frequency = jnp.arange(retained, dtype=jnp.int32)
    phases = frequency[:, None] * positions[None, :] % points
    angles = phases.astype(jnp.float32) * (2.0 * math.pi / points)
    factor = 1.0 / math.sqrt(points)
    cosine_part = jnp.cos(angles) * factor
    sine_part = jnp.sin(angles) * factor
    top_half = jnp.concatenate([cosine_part, sine_part], axis=1)
    low_half = jnp.concatenate([-sine_part, cosine_part], axis=1)
    return jnp.concatenate([top_half, low_half], axis=0).astype(jnp.bfloat16)


def mix_modes(spectrum, first_core, second_core, output_core, input_core):
    count_modes = spectrum.shape[0]
    retained = first_core.shape[0]
    channels = input_core.shape[1]
    unfolded = spectrum.reshape(count_modes, 2, retained, -1, channels)
    joined = jnp.einsum("ka,amb->mkb", first_core, second_core, precision=PRECISE)
    kernel = jnp.einsum("mkb,bdc->mkdc", joined, output_core, precision=PRECISE)
    narrowed = jnp.einsum("ci,mokpi->mokpc", input_core, unfolded, precision=PRECISE)
    widened = jnp.einsum("mkdc,mokpc->mokpd", kernel, narrowed, precision=PRECISE)
    return widened.reshape(spectrum.shape)


def activation(combined):
    cumulative = 0.5 * (1.0 + lax.erf(combined * (1.0 / math.sqrt(2.0))))
    density = jnp.exp(-0.5 * combined * combined) * (1.0 / math.sqrt(2.0 * math.pi))
    return (combined * cumulative, cumulative + combined * density)


def shards(
    field, cotangent, first_core, second_core, output_core, input_core, channel_mix, channel_bias
):
    groups = lax.axis_size("pencil")
    position = lax.axis_index("pencil")
    samples = lax.axis_size("dp")
    source = field[0]
    incoming = cotangent[0]
    slab_rows, slab_cols, features = source.shape
    all_rows = slab_rows * groups
    kept_first = first_core.shape[0]
    kept_local = second_core.shape[1]
    kept_second = kept_local * groups
    channels = input_core.shape[1]
    planes = features // channels
    table_second = build_second(slab_cols, kept_second, slab_cols)
    table_first = build_first(all_rows, kept_first, position * slab_rows, slab_rows)

    def to_spectrum(values):
        expanded = jnp.einsum(
            "xyf,yk->kxf", values, table_second, preferred_element_type=jnp.float32
        ).astype(jnp.bfloat16)
        paired = expanded.reshape(kept_second, 2 * slab_rows, features)
        return lax.psum_scatter(
            jnp.einsum(
                "pq,mqf->mpf", table_first, paired, preferred_element_type=jnp.float32
            ).astype(jnp.bfloat16),
            "pencil",
            scatter_dimension=0,
            tiled=True,
        ).astype(jnp.float32)

    def from_spectrum(modes):
        narrow = modes.astype(jnp.bfloat16)
        portion = lax.all_gather(narrow, "pencil", axis=0, tiled=True)
        expanded = jnp.einsum(
            "pq,mpf->mqf", table_first, portion, preferred_element_type=jnp.float32
        ).astype(jnp.bfloat16)
        expanded = expanded.reshape(2 * portion.shape[0], slab_rows, portion.shape[2])
        return jnp.einsum("kxf,yk->xyf", expanded, table_second, preferred_element_type=jnp.float32)

    wide_mix = jnp.kron(jnp.eye(planes, dtype=jnp.bfloat16), channel_mix)
    spread_bias = jnp.tile(channel_bias, planes)
    spectrum = to_spectrum(source)
    mixed_modes, pullback = jax.vjp(
        mix_modes, spectrum, first_core, second_core, output_core, input_core
    )
    spectral = from_spectrum(mixed_modes)
    flat_source = source.reshape(slab_rows * slab_cols, features)
    direct = jnp.dot(flat_source, wide_mix, preferred_element_type=jnp.float32).reshape(
        slab_rows, slab_cols, features
    )
    combined = direct + spectral + spread_bias
    value, derivative = activation(combined)
    activated = value.astype(jnp.bfloat16)
    upstream = (incoming * derivative).astype(jnp.bfloat16)
    upstream_modes = to_spectrum(upstream)
    returned_modes, first_term, second_term, output_term, input_term = pullback(upstream_modes)
    returned = from_spectrum(returned_modes)
    flat_upstream = upstream.reshape(slab_rows * slab_cols, features)
    back_direct = jnp.dot(flat_upstream, wide_mix.T, preferred_element_type=jnp.float32).reshape(
        slab_rows, slab_cols, features
    )
    field_adjoint = (back_direct + returned).astype(jnp.bfloat16)
    products = jnp.einsum(
        "nf,ng->fg", flat_source, flat_upstream, preferred_element_type=jnp.float32
    )
    mix_term = jnp.einsum("pcpd->cd", products.reshape(planes, channels, planes, channels))
    bias_term = (
        jnp.sum(flat_upstream, axis=0, dtype=jnp.float32).reshape(planes, channels).sum(axis=0)
    )
    summed = lax.psum((first_term, output_term, input_term, mix_term, bias_term), ("dp", "pencil"))
    second_total = lax.psum(second_term, "dp")
    core_scale = 1.0 / math.sqrt(samples * planes * kept_first * kept_second)
    mix_scale = 1.0 / math.sqrt(samples * planes * all_rows * slab_cols)
    return (
        activated[None],
        field_adjoint[None],
        summed[0] * core_scale,
        second_total * core_scale,
        summed[1] * core_scale,
        summed[2] * core_scale,
        summed[3] * mix_scale,
        summed[4] * mix_scale,
    )


def solution(mesh):
    return jax.shard_map(
        shards,
        mesh=mesh,
        in_specs=(
            P("dp", "pencil", None, None),
            P("dp", "pencil", None, None),
            P(),
            P(None, "pencil", None),
            P(),
            P(),
            P(),
            P(),
        ),
        out_specs=(
            P("dp", "pencil", None, None),
            P("dp", "pencil", None, None),
            P(),
            P(None, "pencil", None),
            P(),
            P(),
            P(),
            P(),
        ),
        check_vma=False,
    )
```

profile of v0, /device:TPU:1, one launch (start us, length us, event | category | flops | bytes accessed | tf_op | source)
XLA Modules:
  0.0 643.6 jit_solution(1673376579909043521)
XLA Ops:
  7.2 0.0 copy-start
  7.2 0.0 reduce-scatter.3.cloned.1.call-start
  7.3 0.3 negate_multiply_fusion
  7.5 0.1 fusion.45
  7.7 0.1 copy.102
  7.8 1.0 copy-done
  8.8 0.5 fusion.14
  9.2 0.2 copy.103
  9.4 1.2 fusion.12
  10.6 0.0 reduce-scatter.3.cloned.1.call-update
  10.7 0.0 reduce-scatter.5.cloned.1.call-start
  10.7 0.1 add.81
  10.8 0.1 broadcast_multiply_fusion.1
  11.0 0.1 mul.204
  11.1 2.7 convolution_bitcast_fusion
  13.8 5.6 copy.130
  19.4 0.0 copy-done.5
  19.4 0.2 convolution_bitcast_fusion.7
  19.6 0.0 copy-done.2
  19.6 0.4 convolution_bitcast_fusion.2
  20.1 203.8 %reduce-scatter.3.cloned.1.call-done = bf16[1,64,128]{2,1,0:T(8,128)(2,1)} async-done(((bf16[32,64,128]{2,1,0:T(8,128)(2,1)}), bf16[1,64,128]{2,1,0:T(8,128)(2,1)}) %reduce-scatter.3.cloned.1.call-update) | async-done | bytes 16400 | tf_op jit(solution)/shard_map/reduce_scatter | solution.py:75
  223.8 0.8 reshape.253
  224.7 0.4 fusion.35
  225.0 0.1 copy.106
  225.2 0.5 fusion.17
  225.7 0.1 convert_element_type.144
  225.8 35.7 %all_gather.6 = bf16[32,64,128]{2,1,0:T(8,128)(2,1)S(1)} all-gather(bf16[1,64,128]{2,1,0:T(8,128)(2,1)S(1)} %convert_element_type.144), channel_id=1, replica_groups=mesh['dp'=8,'pencil'=32] {'pencil'}, dimensions={0}, use_global_device_ids=true | all-gather | bytes 540672 | tf_op jit(solution)/shard_map/all_gather | solution.py:86
  261.6 0.3 convolution_convert_fusion.3
  261.8 6.1 convert_reduce_fusion
  267.9 1.3 copy-done.1
  269.3 0.5 convolution_convert_fusion.4
  269.8 0.2 copy.111
  269.9 1.2 fusion.13
  271.1 0.0 reduce-scatter.5.cloned.1.call-update
  271.2 0.1 reshape.272
  271.3 0.1 copy.117
  271.4 0.1 reshape.265
  271.5 2.3 convolution_bitcast_fusion.4
  273.9 0.2 reshape.264
  274.0 0.2 select_reduce_fusion
  274.2 4.2 fusion.51
  278.4 216.9 %reduce-scatter.5.cloned.1.call-done = bf16[1,64,128]{2,1,0:T(8,128)(2,1)} async-done(((bf16[32,64,128]{2,1,0:T(8,128)(2,1)}), bf16[1,64,128]{2,1,0:T(8,128)(2,1)}) %reduce-scatter.5.cloned.1.call-update) | async-done | bytes 16400 | tf_op jit(solution)/shard_map/reduce_scatter | solution.py:75
  495.3 0.8 reshape.258
  496.2 0.5 convolution_bitcast_fusion.3
  496.6 0.1 copy.114
  496.7 0.2 convolution_bitcast_fusion.5
  496.9 0.5 convolution_convert_fusion.5
  497.4 0.4 convolution_bitcast_fusion.1
  497.9 0.4 convolution_bitcast_fusion.8
  498.2 0.4 fusion.22
  498.6 0.1 convolution_bitcast_fusion.6
  498.8 0.1 fusion.52
  498.9 0.1 convert_element_type.155
  499.1 18.1 %psum.43 = f32[16,1,16]{0,2,1:T(8,128)S(1)} all-reduce(f32[16,1,16]{0,2,1:T(8,128)S(1)} %convolution_bitcast_fusion.6), channel_id=1, replica_groups=mesh['dp'=8,'pencil'=32] {'dp'}, use_global_device_ids=true, to_apply=%region_3.4 | all-reduce | flops 256 | bytes 2048 | tf_op jit(solution)/shard_map/psum | solution.py:124
  517.2 0.7 copy.123
  517.8 75.0 %all-reduce = (f32[32,16]{0,1:T(8,128)S(1)}, f32[16,32,16]{1,0,2:T(8,128)S(1)}, f32[16,32]{1,0:T(8,128)S(1)}, f32[32,32]{0,1:T(8,128)S(1)}, f32[32]{0:T(128)S(1)}) all-reduce(f32[32,16]{0,1:T(8,128)S(1)} %fusion.52, f32[16,32,16]{1,0,2:T(8,128)S(1)} %fusion.22, ...), channel_id=1, replica_groups=mesh['dp'=8,'pencil'=32] {'dp','pencil'}, use_global_device_ids=true, to_apply=%region_2.3 | all-reduce | flops 10272 | bytes 82176 | tf_op jit(solution)/shard_map/psum | solution.py:123
  592.8 0.6 broadcast_multiply_fusion.5
  593.4 0.5 broadcast_multiply_fusion.6
  593.9 0.6 broadcast_multiply_fusion.3
  594.5 0.7 copy.125
  595.2 0.7 copy.124
  595.9 36.4 %all_gather.7 = bf16[32,64,128]{2,1,0:T(8,128)(2,1)S(1)} all-gather(bf16[1,64,128]{2,1,0:T(8,128)(2,1)S(1)} %convert_element_type.155), channel_id=1, replica_groups=mesh['dp'=8,'pencil'=32] {'pencil'}, dimensions={0}, use_global_device_ids=true | all-gather | bytes 540672 | tf_op jit(solution)/shard_map/all_gather | solution.py:86
  632.3 0.3 convolution_convert_fusion.2
  632.6 4.2 fusion.11
  (23 shorter events, 0.2 us)
Async XLA Ops:
  7.2 1.6 copy-start
  7.2 3.5 copy-start.7
  7.2 3.6 copy-start.6
  7.2 216.6 %reduce-scatter.3.cloned.1.call-start = ((), (), s32[]{:S(2)}) async-start(), calls=%async_computation.2 | async-start | bytes 540672 | tf_op jit(solution)/shard_map/reduce_scatter | solution.py:75
  10.7 484.7 %reduce-scatter.5.cloned.1.call-start = ((), (), s32[]{:S(2)}) async-start(), calls=%async_computation.3 | async-start | bytes 540672 | tf_op jit(solution)/shard_map/reduce_scatter | solution.py:75
  13.8 5.6 copy-start.4
  13.8 5.6 copy-start.5
  13.8 5.8 copy-start.2
  13.8 210.9 %copy-start.3 = (f32[16,32]{1,0:T(8,128)S(1)}, f32[16,32]{1,0:T(8,128)}, u32[]{:S(2)}) copy-start(f32[16,32]{1,0:T(8,128)} %param.13) | copy-start | bytes 6148
  267.9 1.3 copy-start.1
Sparse Core Ops, SparseCore 0:
  12.4 211.3 reduce-scatter.2
  271.3 224.0 reduce-scatter.4
where the time goes:
time: 654 us; the launch traced here: 644 us
  waiting for transfers between devices  421 us (64%)
  blocking collectives  165 us (25%)
  matrix products  27.6 us (4%)
  between operations  14.3 us (2%)
  local copies, waits for them, and re-layouts  13.2 us (2%)
    reduce_scatter x2, waiting for transfers between devices, to_spectrum(): lax.psum_scatter(jnp.einsum('pq,mqf->mpf', table_first, paired, preferred...  421 us
    psum x1, blocking collectives, shards(): lax.psum((first_term, output_term, input_term, mix_term, bias_term), ('dp...  75 us
    all_gather x2, blocking collectives, from_spectrum(): portion = lax.all_gather(narrow, 'pencil', axis=0, tiled=True)  72.1 us
    psum x1, blocking collectives, shards(): second_total = lax.psum(second_term, 'dp')  18.1 us
  transfers between devices with their start and end apart: 2, of which 2 were waited for; matrix products, arithmetic and copies ran while one was open for 3% of the time, Pallas kernels for 0%

commit v1 on v0

v1 whole, which is shorter than its diff:
```python
import math

import jax
import jax.numpy as jnp
import numpy as np
from jax import lax
from jax.experimental import pallas as pl
from jax.experimental.pallas import tpu as pltpu
from jax.sharding import PartitionSpec as P

F32 = jnp.float32
BF16 = jnp.bfloat16
MESH = pl.DeviceIdType.MESH
HIGHEST = lax.Precision.HIGHEST

NX = 512
NY = 512
C = 32
MX = 32
MY = 32
RANK = 16
PLANES = 4
GROUPS = 8
FEATS = 128
PENCILS = 32
ROWS = NX // PENCILS
HALF = ROWS // 2
MESSAGE = 2 * HALF
BLOCK = PENCILS * MESSAGE
CHUNK = 32
CORE_SCALE = 1.0 / math.sqrt(GROUPS * PLANES * MX * MY)
MIX_SCALE = 1.0 / math.sqrt(GROUPS * PLANES * NX * NY)


def tables():
    y = np.arange(NY, dtype=np.int64)
    m = np.arange(MY, dtype=np.int64)
    angles = (y[:, None] * m[None, :] % NY) * (2.0 * math.pi / NY)
    factor = 1.0 / math.sqrt(NY)
    second = np.stack([np.cos(angles) * factor, -np.sin(angles) * factor], axis=2).reshape(NY, 2 * MY)
    x = np.arange(NX, dtype=np.int64)
    k = np.arange(MX, dtype=np.int64)
    angles = (k[:, None] * x[None, :] % NX) * (2.0 * math.pi / NX)
    factor = 1.0 / math.sqrt(NX)
    a, b = np.cos(angles) * factor, np.sin(angles) * factor
    first = np.concatenate([np.concatenate([a, b], axis=1), np.concatenate([-b, a], axis=1)], axis=0)
    first = first.reshape(2 * MX, 2, PENCILS, 2, HALF).transpose(0, 3, 2, 1, 4).reshape(2 * MX, 2 * NX)
    second = second.astype(np.float32).astype(jnp.bfloat16)
    first = first.astype(np.float32).astype(jnp.bfloat16)
    return second, first


def dot(a, b, precision=None):
    return jnp.dot(a, b, preferred_element_type=F32, precision=precision)


def dot_nt(a, b):
    return lax.dot_general(a, b, (((1,), (1,)), ((), ())), preferred_element_type=F32)


def dot_tn(a, b, precision=None):
    return lax.dot_general(a, b, (((0,), (0,)), ((), ())), preferred_element_type=F32, precision=precision)


def iotas(shape):
    return lax.broadcasted_iota(jnp.int32, shape, 0), lax.broadcasted_iota(jnp.int32, shape, 1)


def select(shape, rule, dtype=F32):
    rows, lanes = iotas(shape)
    return jnp.where(rule(rows, lanes), 1.0, 0.0).astype(dtype)


def kernel(
    field_hbm, cot_hbm, first_core, second_core, output_core, input_core, mix, bias,
    second_t, second, first, first_t,
    act_hbm, adjoint_hbm, grads_out, second_out,
    field, cot, up, stage, scratch, sbuf, rbuf,
    joined_wide, out_wide, in_wide, mix_wide, mix_wide_t, bias_wide, narrow2, zed, spectrum, products,
    gsend, grecv, bsend, brecv, csend,
    load_sem, store_sem, ssem, rsem, gssem, grsem, bssem, brsem, cssem, crsem,
):
    me = lax.axis_index("pencil")
    group = lax.axis_index("dp")

    def load(source, target, slot, x):
        return pltpu.make_async_copy(source.at[pl.ds(x, 4)], target.at[pl.ds(x, 4)], load_sem.at[slot])

    for part in range(4):
        load(field_hbm, field, part, 4 * part).start()
    barrier = pltpu.get_barrier_semaphore()

    def greet(i, carry):
        pl.semaphore_signal(barrier, inc=1, device_id={"pencil": lax.rem(me + 1 + i, PENCILS)}, device_id_type=MESH)
        return carry

    lax.fori_loop(0, PENCILS - 1, greet, 0)

    def greet_group(i, carry):
        pl.semaphore_signal(barrier, inc=1, device_id={"dp": lax.rem(group + 1 + i, GROUPS)}, device_id_type=MESH)
        return carry

    lax.fori_loop(0, GROUPS - 1, greet_group, 0)
    for part in range(4):
        load(cot_hbm, cot, 4 + part, 4 * part).start()

    def send(turn, half):
        def start(i, carry):
            to = lax.rem(me + 1 + i, PENCILS)
            pltpu.make_async_remote_copy(
                src_ref=sbuf.at[turn, half, to],
                dst_ref=rbuf.at[turn, half, me],
                send_sem=ssem.at[turn, half],
                recv_sem=rsem.at[turn, half],
                device_id={"pencil": to},
                device_id_type=MESH,
            ).start()
            return carry

        lax.fori_loop(0, PENCILS - 1, start, 0)
        rbuf[turn, half, me] = sbuf[turn, half, me]

    def whole(turn, half):
        return pltpu.make_async_remote_copy(
            src_ref=sbuf.at[turn, half, pl.ds(0, PENCILS - 1)],
            dst_ref=rbuf.at[turn, half, pl.ds(0, PENCILS - 1)],
            send_sem=ssem.at[turn, half],
            recv_sem=rsem.at[turn, half],
            device_id={"pencil": lax.rem(me + 1, PENCILS)},
            device_id_type=MESH,
        )

    def analyse(source, x, x_half):
        pair = jnp.concatenate([source[x], source[x + 1]], axis=1)
        rows = dot(second_t[...], pair)
        scratch[pl.ds(x_half, 2 * MY, stride=HALF), :] = rows[:, :FEATS]
        scratch[pl.ds(x_half + 1, 2 * MY, stride=HALF), :] = rows[:, FEATS:]
        return rows

    def pack(turn, half):
        sbuf[turn, half] = scratch[...].astype(BF16).reshape(PENCILS, MESSAGE, FEATS)

    for half in range(2):
        for part in range(2):
            load(field_hbm, field, 2 * half + part, HALF * half + 4 * part).wait()
            for x in range(4 * part, 4 * part + 4, 2):
                analyse(field, HALF * half + x, x)
        pack(0, half)
        if half == 0:
            pl.semaphore_wait(barrier, PENCILS + GROUPS - 2)
        send(0, half)

    joined = dot(first_core[...], second_core[...], HIGHEST)
    joined2 = jnp.concatenate([joined, joined], axis=0)
    spread = select((RANK, 1024), lambda r, l: r == 2 * (l // 128) + (l % 128) // 64)
    joined_wide[...] = dot(joined2, spread, HIGHEST)
    to_pairs = select((RANK, FEATS), lambda r, l: r == l % RANK, BF16)
    out_pairs = dot(output_core[...].astype(BF16), to_pairs)
    _, lanes32 = iotas((C, FEATS))
    rows128, lanes128 = iotas((FEATS, FEATS))
    keep = (rows128 // C) == (lanes128 % 64) // RANK
    for beta in range(RANK // 2):
        low = out_pairs[2 * C * beta : 2 * C * beta + C]
        high = out_pairs[2 * C * beta + C : 2 * C * beta + 2 * C]
        one = jnp.where(lanes32 < 64, low, high)
        tiled = jnp.concatenate([one] * PLANES, axis=0)
        out_wide[:, 128 * beta : 128 * beta + 128] = jnp.where(keep, tiled, 0.0).astype(BF16)
    to_lanes = select((C, FEATS), lambda r, l: r == l % C, BF16)
    to_rows = select((FEATS, C), lambda r, l: r % C == l, BF16)
    pair_rows = select((FEATS, RANK), lambda r, l: r % RANK == l, BF16)
    in_rows = dot(pair_rows, input_core[...].astype(BF16)).astype(BF16)
    in_keep = (rows128 % 64) // RANK == lanes128 // C
    in_wide[...] = jnp.where(in_keep, dot(in_rows, to_lanes), 0.0).astype(BF16)
    same = rows128 // C == lanes128 // C
    mix_rows = dot(to_rows, mix[...]).astype(BF16)
    mix_wide[...] = jnp.where(same, dot(mix_rows, to_lanes), 0.0).astype(BF16)
    mix_rows = dot_nt(to_rows, mix[...]).astype(BF16)
    mix_wide_t[...] = jnp.where(same, dot(mix_rows, to_lanes), 0.0).astype(BF16)
    bias_wide[...] = dot(bias[...], to_lanes.astype(F32), HIGHEST)

    def gather_modes(turn):
        total = None
        for half in range(2):
            whole(turn, half).wait_recv()
            term = dot(first[:, BLOCK * half : BLOCK * (half + 1)], rbuf[turn, half].reshape(BLOCK, FEATS))
            total = term if total is None else total + term
        return total

    def scatter_modes(turn, modes):
        narrow = modes.astype(BF16)
        for half in range(2):
            rows = dot(first_t[BLOCK * half : BLOCK * (half + 1), :], narrow)
            sbuf[turn, half] = rows.astype(BF16).reshape(PENCILS, MESSAGE, FEATS)
            send(turn, half)

    modes = gather_modes(0)
    spectrum[...] = modes
    doubled = dot_nt(modes.astype(BF16), in_wide[...])
    narrow2[...] = doubled
    for beta in range(RANK // 2):
        cols = slice(128 * beta, 128 * beta + 128)
        zed[:, cols] = (joined_wide[:, cols] * doubled).astype(BF16)
    scatter_modes(1, dot_nt(zed[...], out_wide[...]))

    def unpack(turn, half):
        whole(turn, half).wait_recv()
        scratch[...] = rbuf[turn, half].astype(F32).reshape(BLOCK, FEATS)

    def store(source, target, slot, x):
        return pltpu.make_async_copy(source.at[pl.ds(x, 4)], target.at[pl.ds(x, 4)], store_sem.at[slot])

    bias_row = bias_wide[...]
    for part in range(4):
        load(cot_hbm, cot, 4 + part, 4 * part).wait()

    def activate(x, rows_x):
        rhs = jnp.concatenate([mix_wide[...], rows_x], axis=0)
        for y in range(0, NY, 128):
            lhs = jnp.concatenate([field[x, y : y + 128], second[y : y + 128]], axis=1)
            combined = dot(lhs, rhs) + bias_row
            cumulative = 0.5 + 0.5 * lax.erf(combined * math.sqrt(0.5))
            density = jnp.exp(-0.5 * combined * combined) * (1.0 / math.sqrt(2.0 * math.pi))
            stage[x, y : y + 128] = (combined * cumulative).astype(BF16)
            derivative = cumulative + combined * density
            up[x, y : y + 128] = (cot[x, y : y + 128].astype(F32) * derivative).astype(BF16)

    rows_sum = jnp.zeros((1, FEATS), F32)
    for half in range(2):
        unpack(1, half)
        base = HALF * half

        def body(j, carry, base=base):
            for s in range(2):
                x = 2 * j + s
                rows_x = scratch[pl.ds(x, 2 * MY, stride=HALF), :].astype(BF16)
                activate(base + x, rows_x)
            return carry

        lax.fori_loop(0, HALF // 2, body, 0)
        for part in range(2):
            store(stage, act_hbm, 2 * half + part, base + 4 * part).start()
        for x in range(0, HALF, 2):
            rows = analyse(up, base + x, x)
            rows_sum = rows_sum + rows[0:1, :FEATS] + rows[0:1, FEATS:]
        pack(2, half)
        send(2, half)

    products[...] = jnp.zeros_like(products)

    def accumulate(x, carry):
        products[...] += dot_tn(field[x], up[x])
        return carry

    lax.fori_loop(0, ROWS, accumulate, 0)
    folded = jnp.where(same, products[...], 0.0)
    folded = folded[0:32] + folded[32:64] + folded[64:96] + folded[96:128]
    fold_low = select((FEATS, FEATS), lambda r, l: r % C == l)
    mix_part = dot(folded, fold_low, HIGHEST)
    fold_high = select((FEATS, FEATS), lambda r, l: r % C + 64 == l)
    unit = np.float32(np.asarray(1.0 / math.sqrt(NY), dtype=np.float32).astype(jnp.bfloat16))
    bias_part = dot(rows_sum * (1.0 / float(unit)), fold_high, HIGHEST)

    upstream = gather_modes(2)
    upstream_b = upstream.astype(BF16)
    dz = dot(upstream_b, out_wide[...])
    weighted = joined_wide[...] * dz
    dn = weighted[:, 0:128]
    for beta in range(1, RANK // 2):
        dn = dn + weighted[:, 128 * beta : 128 * beta + 128]
    dn_b = dn.astype(BF16)
    scatter_modes(3, dot(dn_b, in_wide[...]))

    fold_rank = select((1024, RANK), lambda r, l: l == 2 * (r // 128) + (r % 128) // 64, BF16)
    product = jnp.concatenate(
        [dz[:, 128 * b : 128 * b + 128] * narrow2[...] for b in range(RANK // 2)], axis=1
    ).astype(BF16)
    djoined = dot(product, fold_rank)
    djoined = djoined[:MX] + djoined[MX:]
    place = select((RANK, FEATS), lambda r, l: l == r + 32)
    first_part = dot(djoined, dot_tn(second_core[...], place, HIGHEST), HIGHEST)
    second_part = dot(dot_tn(first_core[...], djoined, HIGHEST), select((RANK, FEATS), lambda r, l: l == r), HIGHEST)
    outer = dot_tn(upstream_b, zed[...])
    halves = []
    for high in range(2):
        total = None
        for low in range(4):
            beta = 4 * high + low
            block = jnp.where(keep, outer[:, 128 * beta : 128 * beta + 128], 0.0)
            block = (block[0:32] + block[32:64] + block[64:96] + block[96:128]).astype(BF16)
            fold = select(
                (FEATS, FEATS), lambda r, l, low=low: l == low * 32 + (r // 64) * RANK + r % RANK, BF16
            )
            term = dot(block, fold)
            total = term if total is None else total + term
        halves.append(total)
    inner = jnp.where(in_keep, dot_tn(dn_b, spectrum[...].astype(BF16)), 0.0)
    inner = sum(inner[RANK * i : RANK * (i + 1)] for i in range(1, 2 * PLANES)) + inner[0:RANK]
    input_part = dot(inner, fold_high, HIGHEST)
    misc = (mix_part * (MIX_SCALE / CORE_SCALE) + first_part) + jnp.concatenate(
        [input_part, bias_part * (MIX_SCALE / CORE_SCALE), jnp.zeros((15, FEATS), F32)], axis=0
    )
    for q in range(GROUPS):
        gsend[q, 0:8] = halves[q // 4][8 * (q % 4) : 8 * (q % 4) + 8]
        gsend[q, 8:12] = misc[4 * q : 4 * q + 4]
        gsend[q, 12:16] = jnp.zeros((4, FEATS), F32)
        gsend[q, 16:32] = second_part

    def start_groups(i, carry):
        to = lax.rem(group + 1 + i, GROUPS)
        pltpu.make_async_remote_copy(
            src_ref=gsend.at[to], dst_ref=grecv.at[group], send_sem=gssem, recv_sem=grsem,
            device_id={"dp": to}, device_id_type=MESH,
        ).start()
        return carry

    def all_groups(source, target, sent, received):
        return pltpu.make_async_remote_copy(
            src_ref=source, dst_ref=target, send_sem=sent, recv_sem=received,
            device_id={"dp": lax.rem(group + 1, GROUPS)}, device_id_type=MESH,
        )

    lax.fori_loop(0, GROUPS - 1, start_groups, 0)
    grecv[group] = gsend[group]
    seven = pl.ds(0, GROUPS - 1)
    all_groups(gsend.at[seven], grecv.at[seven], gssem, grsem).wait_recv()
    chunk = grecv[0]
    for q in range(1, GROUPS):
        chunk = chunk + grecv[q]
    second_out[...] = chunk[16:32] * CORE_SCALE
    bsend[...] = chunk[0:16].astype(BF16)

    def start_pencils(i, carry):
        to = lax.rem(me + 1 + i, PENCILS)
        pltpu.make_async_remote_copy(
            src_ref=bsend, dst_ref=brecv.at[me], send_sem=bssem, recv_sem=brsem,
            device_id={"pencil": to}, device_id_type=MESH,
        ).start()
        return carry

    lax.fori_loop(0, PENCILS - 1, start_pencils, 0)
    brecv[me] = bsend[...]

    def finish(x, rows_x):
        rhs = jnp.concatenate([mix_wide_t[...], rows_x], axis=0)
        for y in range(0, NY, 128):
            lhs = jnp.concatenate([up[x, y : y + 128], second[y : y + 128]], axis=1)
            cot[x, y : y + 128] = dot(lhs, rhs).astype(BF16)

    def finish_half(half):
        unpack(3, half)
        base = HALF * half

        def body(j, carry):
            for s in range(2):
                x = 2 * j + s
                rows_x = scratch[pl.ds(x, 2 * MY, stride=HALF), :].astype(BF16)
                finish(base + x, rows_x)
            return carry

        lax.fori_loop(0, HALF // 2, body, 0)
        for part in range(2):
            store(cot, adjoint_hbm, 4 + 2 * half + part, base + 4 * part).start()

    finish_half(0)
    finish_half(1)

    thirtyone = pl.ds(0, PENCILS - 1)
    pltpu.make_async_remote_copy(
        src_ref=brecv.at[thirtyone], dst_ref=brecv.at[thirtyone], send_sem=bssem, recv_sem=brsem,
        device_id={"pencil": lax.rem(me + 1, PENCILS)}, device_id_type=MESH,
    ).wait_recv()
    total = brecv[0].astype(F32)
    for q in range(1, PENCILS):
        total = total + brecv[q].astype(F32)
    csend[...] = total * CORE_SCALE

    def start_last(i, carry):
        to = lax.rem(group + 1 + i, GROUPS)
        pltpu.make_async_remote_copy(
            src_ref=csend, dst_ref=grads_out.at[group], send_sem=cssem, recv_sem=crsem,
            device_id={"dp": to}, device_id_type=MESH,
        ).start()
        return carry

    lax.fori_loop(0, GROUPS - 1, start_last, 0)
    grads_out[group] = csend[...]
    last = all_groups(grads_out.at[seven], grads_out.at[seven], cssem, crsem)
    last.wait_recv()

    last.wait_send()
    all_groups(gsend.at[seven], grecv.at[seven], gssem, grsem).wait_send()
    pltpu.make_async_remote_copy(
        src_ref=brecv.at[thirtyone], dst_ref=brecv.at[thirtyone], send_sem=bssem, recv_sem=brsem,
        device_id={"pencil": lax.rem(me + 1, PENCILS)}, device_id_type=MESH,
    ).wait_send()
    for turn in range(4):
        for half in range(2):
            whole(turn, half).wait_send()
    for part in range(4):
        store(stage, act_hbm, part, 4 * part).wait()
        store(cot, adjoint_hbm, 4 + part, 4 * part).wait()


def shards(field, cotangent, first_core, second_core, output_core, input_core, channel_mix, channel_bias):
    second, first = tables()
    slab = (ROWS, NY, FEATS)
    vmem = pl.BlockSpec(memory_space=pltpu.VMEM)
    anywhere = pl.BlockSpec(memory_space=pl.ANY)
    dma = pltpu.SemaphoreType.DMA
    act, adjoint, grads, second_total = pl.pallas_call(
        kernel,
        out_shape=[
            jax.ShapeDtypeStruct(slab, BF16),
            jax.ShapeDtypeStruct(slab, BF16),
            jax.ShapeDtypeStruct((GROUPS, 16, FEATS), F32),
            jax.ShapeDtypeStruct((16, FEATS), F32),
        ],
        in_specs=[anywhere, anywhere] + [vmem] * 10,
        out_specs=[anywhere, anywhere, vmem, vmem],
        scratch_shapes=[
            pltpu.VMEM(slab, BF16),
            pltpu.VMEM(slab, BF16),
            pltpu.VMEM(slab, BF16),
            pltpu.VMEM(slab, BF16),
            pltpu.VMEM((BLOCK, FEATS), F32),
            pltpu.VMEM((4, 2, PENCILS, MESSAGE, FEATS), BF16),
            pltpu.VMEM((4, 2, PENCILS, MESSAGE, FEATS), BF16),
            pltpu.VMEM((2 * MX, 1024), F32),
            pltpu.VMEM((FEATS, 1024), BF16),
            pltpu.VMEM((FEATS, FEATS), BF16),
            pltpu.VMEM((FEATS, FEATS), BF16),
            pltpu.VMEM((FEATS, FEATS), BF16),
            pltpu.VMEM((1, FEATS), F32),
            pltpu.VMEM((2 * MX, FEATS), F32),
            pltpu.VMEM((2 * MX, 1024), BF16),
            pltpu.VMEM((2 * MX, FEATS), F32),
            pltpu.VMEM((FEATS, FEATS), F32),
            pltpu.VMEM((GROUPS, CHUNK, FEATS), F32),
            pltpu.VMEM((GROUPS, CHUNK, FEATS), F32),
            pltpu.VMEM((16, FEATS), BF16),
            pltpu.VMEM((PENCILS, 16, FEATS), BF16),
            pltpu.VMEM((16, FEATS), F32),
            dma((8,)),
            dma((8,)),
            dma((4, 2)),
            dma((4, 2)),
            dma,
            dma,
            dma,
            dma,
            dma,
            dma,
        ],
        compiler_params=pltpu.CompilerParams(
            collective_id=0, has_side_effects=True, vmem_limit_bytes=48 * 2**20
        ),
    )(
        field[0],
        cotangent[0],
        first_core,
        second_core[:, 0, :],
        output_core.reshape(RANK * C, RANK),
        input_core,
        channel_mix,
        channel_bias[None],
        np.ascontiguousarray(second.T),
        second,
        first,
        np.ascontiguousarray(first.T),
    )
    outer = grads[:, 0:8].reshape(2, C, 8, RANK).transpose(0, 2, 1, 3).reshape(RANK, C, RANK)
    misc = grads[:, 8:12].reshape(C, FEATS)
    return (
        act[None],
        adjoint[None],
        misc[:, 32 : 32 + RANK],
        second_total[:, None, :RANK],
        outer,
        misc[:RANK, 64 : 64 + C],
        misc[:, :C],
        misc[RANK, 64 : 64 + C],
    )


def solution(mesh):
    slabs = P("dp", "pencil", None, None)
    column = P(None, "pencil", None)
    return jax.shard_map(
        shards,
        mesh=mesh,
        in_specs=(slabs, slabs, P(), column, P(), P(), P(), P()),
        out_specs=(slabs, slabs, P(), column, P(), P(), P(), P()),
        check_vma=False,
    )
```

time: 654 us -> 76.2 us (0.12); the launches traced: 644 us -> 75.8 us
  waiting for transfers between devices: 421 us -> 0 us
  blocking collectives: 165 us -> 0 us
  Pallas kernels: 0 us -> 57.7 us
  matrix products: 27.6 us -> 0 us
  between operations: 14.3 us -> 0.69 us
    reduce_scatter x2 -> x0, waiting for transfers between devices: 421 us -> none  [to_spectrum(): lax.psum_scatter(jnp.einsum('pq,mqf->mpf', table_first, paired, preferred...]
    psum x2 -> x0, blocking collectives: 93 us -> none  [the longest x1 75 us: shards(): lax.psum((first_term, output_term, input_term, mix_term, bias_term), ('dp...]
    all_gather x2 -> x0, blocking collectives: 72.1 us -> none  [from_spectrum(): portion = lax.all_gather(narrow, 'pencil', axis=0, tiled=True)]
    pallas_call x0 -> x1, Pallas kernels: none -> 57.7 us  [shards(): pl.pallas_call(kernel, out_shape=[jax.ShapeDtypeStruct(slab, BF16), jax.S...]
    dot_general x23 -> x0, matrix products: 27.6 us -> none  [the longest x2 10.3 us: from_spectrum(): jnp.einsum('kxf,yk->xyf', expanded, table_second, preferred_element_type=...]
    unnamed x19 -> x26, local copies, waits for them, and re-layouts: 4.35 us -> 15.2 us
    reshape x4 -> x1, local copies, waits for them, and re-layouts: 6.68 us -> 0.12 us  [shards(): grads[:, 0:8].reshape(2, C, 8, RANK).transpose(0, 2, 1, 3)]
  transfers between devices with their start and end apart: 2 -> 0, of which waited for: 2 -> 0; matrix products, arithmetic and copies ran while one was open for 3% -> 0% of each run, Pallas kernels for 0% -> 0%
where the time goes in v1:
time: 76.2 us; the launch traced here: 75.8 us
  Pallas kernels  57.7 us (76%)
  local copies, waits for them, and re-layouts  17.4 us (23%)
    pallas_call x1, Pallas kernels, shards(): pl.pallas_call(kernel, out_shape=[jax.ShapeDtypeStruct(slab, BF16), jax.S...  57.7 us
    unnamed x26, local copies, waits for them, and re-layouts  15.2 us

profile of v1, /device:TPU:1, one launch (start us, length us, event | category | flops | bytes accessed | tf_op | source)
XLA Modules:
  0.0 75.8 jit_solution(7401720790936487943)
XLA Ops:
  0.6 0.8 %copy.30.first_core = f32[32,16]{1,0:T(8,128)S(1)} copy(f32[32,16]{0,1:T(8,128)} %param.14) | data formatting | bytes 4096 | tf_op args[2]
  1.4 1.0 %copy.29 = f32[16,32,16]{2,1,0:T(8,128)S(1)} copy(f32[16,32,16]{1,2,0:T(8,128)} %param.16) | data formatting | bytes 65536 | tf_op args[4]
  2.4 0.0 copy-start.1
  2.5 0.9 %copy-done.1 = bf16[1024,64]{1,0:T(8,128)(2,1)S(1)} copy-done((bf16[1024,64]{1,0:T(8,128)(2,1)S(1)}, bf16[1024,64]{1,0:T(8,128)(2,1)}, u32[]{:S(2)}) %copy-start.1) | copy-done | bytes 131096
  3.4 0.0 copy-start.2
  3.4 0.9 %copy-done.2 = bf16[64,1024]{1,0:T(8,128)(2,1)S(1)} copy-done((bf16[64,1024]{1,0:T(8,128)(2,1)S(1)}, bf16[64,1024]{1,0:T(8,128)(2,1)}, u32[]{:S(2)}) %copy-start.2) | copy-done | bytes 131096
  4.3 0.0 copy-start.3
  4.3 0.9 %copy-done.3 = bf16[512,64]{1,0:T(8,128)(2,1)S(1)} copy-done((bf16[512,64]{1,0:T(8,128)(2,1)S(1)}, bf16[512,64]{1,0:T(8,128)(2,1)}, u32[]{:S(2)}) %copy-start.3) | copy-done | bytes 65560
  5.2 0.0 copy-start.4
  5.2 0.8 %copy-done.4 = bf16[64,512]{1,0:T(8,128)(2,1)S(1)} copy-done((bf16[64,512]{1,0:T(8,128)(2,1)S(1)}, bf16[64,512]{1,0:T(8,128)(2,1)}, u32[]{:S(2)}) %copy-start.4) | copy-done | bytes 65560
  6.0 0.0 copy-start.5
  6.0 0.7 copy-done.5
  6.7 0.0 copy-start.6
  6.7 0.7 copy-done.6
  7.4 0.0 copy-start.7
  7.4 0.7 copy-done.7
  8.1 0.0 copy-start.8
  8.1 0.7 copy-done.8
  8.8 57.7 %shard_map.179 = (bf16[16,512,128]{2,1,0:T(8,128)(2,1)S(1)}, bf16[16,512,128]{2,1,0:T(8,128)(2,1)S(1)}, f32[8,16,128]{2,1,0:T(8,128)S(1)}, f32[16,128]{1,0:T(8,128)S(1)}) custom-call(bf16[16,512,128]{2,1,0:T(8,128)(2,1)} %bitcast.23, bf16[16,512,128]{2,1,0:T(8,128)(2,1)} %bitcast.24, f32[32,16]{1,0:T(8,128)S(1)} %copy.30.first_core, f32[16,16]{1,0:T(8,128)S(1)} %bitcast.20, ...), custom_call_target="tpu_custom_call" | custom-call | tf_op jit(solution)/shard_map/pallas_call | solution.py:410
  66.5 0.0 copy-start
  66.5 1.3 %copy-done = bf16[16,512,128]{2,1,0:T(8,128)(2,1)} copy-done((bf16[16,512,128]{2,1,0:T(8,128)(2,1)}, bf16[16,512,128]{2,1,0:T(8,128)(2,1)S(1)}, u32[]{:S(2)}) %copy-start) | copy-done | bytes 2097176
  67.8 0.0 copy-start.9
  67.8 0.6 slice_bitcast_fusion
  68.4 0.7 slice.29
  69.0 0.1 slice.28
  69.1 0.7 copy.32
  69.8 0.1 reshape.30
  69.9 0.8 %copy.31 = f32[2,8,32,16]{2,3,1,0:T(8,128)} copy(f32[2,8,32,16]{3,1,2,0:T(8,128)S(1)} %bitcast.25) | data formatting | bytes 65536 | tf_op jit(solution)/shard_map/transpose | solution.py:471
  70.7 3.1 %copy.37 = bf16[1,16,512,128]{3,2,1,0:T(8,128)(2,1)} copy(bf16[1,16,512,128]{3,2,1,0:T(8,128)(2,1)} %bitcast.18) | data formatting | bytes 4194304
  73.8 0.0 copy-done.9
  73.8 1.3 %copy.38 = bf16[1,16,512,128]{3,2,1,0:T(8,128)(2,1)} copy(bf16[1,16,512,128]{3,2,1,0:T(8,128)(2,1)S(1)} %bitcast.17) | data formatting | bytes 4194304
  75.2 0.6 copy.39
  (2 shorter events, 0.0 us)
Async XLA Ops:
  2.4 1.0 %copy-start.1 = (bf16[1024,64]{1,0:T(8,128)(2,1)S(1)}, bf16[1024,64]{1,0:T(8,128)(2,1)}, u32[]{:S(2)}) copy-start(bf16[1024,64]{1,0:T(8,128)(2,1)} %constant.11.clone.first_t) | copy-start | bytes 393220
  3.4 0.9 %copy-start.2 = (bf16[64,1024]{1,0:T(8,128)(2,1)S(1)}, bf16[64,1024]{1,0:T(8,128)(2,1)}, u32[]{:S(2)}) copy-start(bf16[64,1024]{1,0:T(8,128)(2,1)} %constant.10.clone.first) | copy-start | bytes 393220
  4.3 0.9 %copy-start.3 = (bf16[512,64]{1,0:T(8,128)(2,1)S(1)}, bf16[512,64]{1,0:T(8,128)(2,1)}, u32[]{:S(2)}) copy-start(bf16[512,64]{1,0:T(8,128)(2,1)} %constant.9.clone.second) | copy-start | bytes 196612
  5.2 0.8 %copy-start.4 = (bf16[64,512]{1,0:T(8,128)(2,1)S(1)}, bf16[64,512]{1,0:T(8,128)(2,1)}, u32[]{:S(2)}) copy-start(bf16[64,512]{1,0:T(8,128)(2,1)} %constant.8.clone.second_t) | copy-start | bytes 196612
  6.0 0.7 copy-start.5
  6.7 0.7 copy-start.6
  7.4 0.7 copy-start.7
  8.1 0.7 copy-start.8
  66.5 1.3 %copy-start = (bf16[16,512,128]{2,1,0:T(8,128)(2,1)}, bf16[16,512,128]{2,1,0:T(8,128)(2,1)S(1)}, u32[]{:S(2)}) copy-start(bf16[16,512,128]{2,1,0:T(8,128)(2,1)S(1)} %get-tuple-element.12) | copy-start | bytes 6291460
  67.8 6.0 %copy-start.9 = (f32[8,4,128]{2,1,0:T(4,128)}, f32[8,4,128]{2,1,0:T(4,128)S(1)}, u32[]{:S(2)}) copy-start(f32[8,4,128]{2,1,0:T(4,128)S(1)} %slice.21) | copy-start | bytes 49156

commit v2 on v1

v2 whole, which is shorter than its diff:
```python
import math

import jax
import jax.numpy as jnp
import numpy as np
from jax import lax
from jax.experimental import pallas as pl
from jax.experimental.pallas import tpu as pltpu
from jax.sharding import PartitionSpec as P

F32 = jnp.float32
BF16 = jnp.bfloat16
MESH = pl.DeviceIdType.MESH
HIGHEST = lax.Precision.HIGHEST

NX = 512
NY = 512
C = 32
MX = 32
MY = 32
RANK = 16
PLANES = 4
GROUPS = 8
FEATS = 128
PENCILS = 32
ROWS = NX // PENCILS
HALF = ROWS // 2
MESSAGE = 2 * HALF
BLOCK = PENCILS * MESSAGE
CHUNK = 32
STOP = 13
CORE_SCALE = 1.0 / math.sqrt(GROUPS * PLANES * MX * MY)
MIX_SCALE = 1.0 / math.sqrt(GROUPS * PLANES * NX * NY)


def tables():
    y = np.arange(NY, dtype=np.int64)
    m = np.arange(MY, dtype=np.int64)
    angles = (y[:, None] * m[None, :] % NY) * (2.0 * math.pi / NY)
    factor = 1.0 / math.sqrt(NY)
    second = np.stack([np.cos(angles) * factor, -np.sin(angles) * factor], axis=2).reshape(NY, 2 * MY)
    x = np.arange(NX, dtype=np.int64)
    k = np.arange(MX, dtype=np.int64)
    angles = (k[:, None] * x[None, :] % NX) * (2.0 * math.pi / NX)
    factor = 1.0 / math.sqrt(NX)
    a, b = np.cos(angles) * factor, np.sin(angles) * factor
    first = np.concatenate([np.concatenate([a, b], axis=1), np.concatenate([-b, a], axis=1)], axis=0)
    first = first.reshape(2 * MX, 2, PENCILS, 2, HALF).transpose(0, 3, 2, 1, 4).reshape(2 * MX, 2 * NX)
    pad = np.zeros((NY, FEATS - 2 * MY))
    pieces = (
        [second[FEATS * i : FEATS * (i + 1)].T for i in range(NY // FEATS)]
        + [first[:, FEATS * i : FEATS * (i + 1)] for i in range(2 * NX // FEATS)]
        + [np.concatenate([second, pad], axis=1)]
        + [np.concatenate([first.T, np.concatenate([pad, pad])], axis=1)]
    )
    return np.concatenate(pieces, axis=0).astype(np.float32).astype(jnp.bfloat16)


def dot(a, b, precision=None):
    return jnp.dot(a, b, preferred_element_type=F32, precision=precision)


def dot_nt(a, b):
    return lax.dot_general(a, b, (((1,), (1,)), ((), ())), preferred_element_type=F32)


def dot_tn(a, b, precision=None):
    return lax.dot_general(a, b, (((0,), (0,)), ((), ())), preferred_element_type=F32, precision=precision)


def iotas(shape):
    return lax.broadcasted_iota(jnp.int32, shape, 0), lax.broadcasted_iota(jnp.int32, shape, 1)


def select(shape, rule, dtype=F32):
    rows, lanes = iotas(shape)
    return jnp.where(rule(rows, lanes), 1.0, 0.0).astype(dtype)


def kernel(
    field_hbm, cot_hbm, first_hbm, second_hbm, output_hbm, input_hbm, mix_hbm, bias_hbm, table_hbm,
    act, adjoint, grads_out, second_out,
    field, cot, up, scratch, sbuf, rbuf,
    first_core, second_core, output_core, input_core, mix, bias, second_t, first, second, first_t,
    joined_wide, out_wide, in_wide, mix_wide, mix_wide_t, bias_wide, narrow2, zed, spectrum, products, rows_sum,
    gsend, grecv, bsend, brecv, csend,
    load_sem, small_sem, ssem, rsem, gssem, grsem, bssem, brsem, cssem, crsem,
):
    me = lax.axis_index("pencil")
    group = lax.axis_index("dp")

    def load(source, target, slot, x):
        return pltpu.make_async_copy(source.at[pl.ds(x, 4)], target.at[pl.ds(x, 4)], load_sem.at[slot])

    smalls = []
    for i in range(NY // FEATS):
        smalls.append((table_hbm.at[pl.ds(64 * i, 64)], second_t.at[:, pl.ds(FEATS * i, FEATS)]))
    for i in range(2 * NX // FEATS):
        smalls.append((table_hbm.at[pl.ds(256 + 64 * i, 64)], first.at[:, pl.ds(FEATS * i, FEATS)]))
    smalls.append((table_hbm.at[pl.ds(768, NY)], second))
    smalls.append((table_hbm.at[pl.ds(768 + NY, 2 * NX)], first_t))
    smalls += [
        (first_hbm, first_core), (second_hbm, second_core), (output_hbm, output_core),
        (input_hbm, input_core), (mix_hbm, mix), (bias_hbm, bias),
    ]
    copies = [pltpu.make_async_copy(a, b, small_sem.at[i]) for i, (a, b) in enumerate(smalls)]

    for copy in copies[:4]:
        copy.start()
    load(field_hbm, field, 0, 0).start()
    barrier = pltpu.get_barrier_semaphore()

    def greet(i, carry):
        pl.semaphore_signal(barrier, inc=1, device_id={"pencil": lax.rem(me + 1 + i, PENCILS)}, device_id_type=MESH)
        return carry

    lax.fori_loop(0, PENCILS - 1, greet, 0)

    def greet_group(i, carry):
        pl.semaphore_signal(barrier, inc=1, device_id={"dp": lax.rem(group + 1 + i, GROUPS)}, device_id_type=MESH)
        return carry

    lax.fori_loop(0, GROUPS - 1, greet_group, 0)
    for part in range(1, 4):
        load(field_hbm, field, part, 4 * part).start()
    for copy in copies[4:]:
        copy.start()
    for part in range(4):
        load(cot_hbm, cot, 4 + part, 4 * part).start()

    def send(turn, half):
        def start(i, carry):
            to = lax.rem(me + 1 + i, PENCILS)
            pltpu.make_async_remote_copy(
                src_ref=sbuf.at[turn, half, to],
                dst_ref=rbuf.at[turn, half, me],
                send_sem=ssem.at[turn, half],
                recv_sem=rsem.at[turn, half],
                device_id={"pencil": to},
                device_id_type=MESH,
            ).start()
            return carry

        lax.fori_loop(0, PENCILS - 1, start, 0)
        rbuf[turn, half, me] = sbuf[turn, half, me]

    def whole(turn, half):
        return pltpu.make_async_remote_copy(
            src_ref=sbuf.at[turn, half, pl.ds(0, PENCILS - 1)],
            dst_ref=rbuf.at[turn, half, pl.ds(0, PENCILS - 1)],
            send_sem=ssem.at[turn, half],
            recv_sem=rsem.at[turn, half],
            device_id={"pencil": lax.rem(me + 1, PENCILS)},
            device_id_type=MESH,
        )

    def analyse(source, x, x_half):
        pair = jnp.concatenate([source[x], source[x + 1]], axis=1)
        rows = dot(second_t[...], pair)
        scratch[pl.ds(x_half, 2 * MY, stride=HALF), :] = rows[:, :FEATS]
        scratch[pl.ds(x_half + 1, 2 * MY, stride=HALF), :] = rows[:, FEATS:]
        return rows

    def pack(turn, half):
        sbuf[turn, half] = scratch[...].astype(BF16).reshape(PENCILS, MESSAGE, FEATS)

    def gather_modes(turn):
        total = None
        for half in range(2):
            whole(turn, half).wait_recv()
            term = dot(first[:, BLOCK * half : BLOCK * (half + 1)], rbuf[turn, half].reshape(BLOCK, FEATS))
            total = term if total is None else total + term
        return total

    def scatter_modes(turn, modes):
        narrow = modes.astype(BF16)
        for half in range(2):
            rows = dot(first_t[BLOCK * half : BLOCK * (half + 1), : 2 * MX], narrow)
            sbuf[turn, half] = rows.astype(BF16).reshape(PENCILS, MESSAGE, FEATS)
            send(turn, half)

    def unpack(turn, half):
        whole(turn, half).wait_recv()
        scratch[...] = rbuf[turn, half].astype(F32).reshape(BLOCK, FEATS)

    rows128, lanes128 = iotas((FEATS, FEATS))
    same = rows128 // C == lanes128 // C
    in_keep = (rows128 % 64) // RANK == lanes128 // C

    def field_rows():
        for copy in copies[:4]:
            copy.wait()
        for half in range(2):
            for part in range(2):
                load(field_hbm, field, 2 * half + part, HALF * half + 4 * part).wait()
                for x in range(4 * part, 4 * part + 4, 2):
                    analyse(field, HALF * half + x, x)
            pack(0, half)
            if half == 0:
                pl.semaphore_wait(barrier, PENCILS + GROUPS - 2)
            send(0, half)

    def weights():
        for copy in copies[4:]:
            copy.wait()
        joined = dot_tn(first_core[...], second_core[...], HIGHEST)
        joined2 = jnp.concatenate([joined, joined], axis=0)
        spread = select((RANK, 1024), lambda r, l: r == 2 * (l // 128) + (l % 128) // 64)
        joined_wide[...] = dot(joined2, spread, HIGHEST)
        to_lanes = select((C, FEATS), lambda r, l: r == l % C, BF16)
        to_rows = select((FEATS, C), lambda r, l: r % C == l, BF16)
        pair_rows = select((FEATS, RANK), lambda r, l: r % RANK == l, BF16)
        for beta in range(RANK // 2):
            rows = output_core[2 * RANK * beta : 2 * RANK * beta + 2 * RANK].astype(BF16)
            low, high = rows[:RANK], rows[RANK:]
            tall = jnp.concatenate([low] * PLANES + [high] * PLANES, axis=0)
            wide = jnp.where(in_keep, dot(tall, to_lanes), 0.0)
            out_wide[128 * beta : 128 * beta + 128, :] = wide.astype(BF16)
        in_rows = dot(pair_rows, input_core[...].astype(BF16)).astype(BF16)
        in_wide[...] = jnp.where(in_keep, dot(in_rows, to_lanes), 0.0).astype(BF16)
        mix_rows = dot(to_rows, mix[...]).astype(BF16)
        mix_wide[...] = jnp.where(same, dot(mix_rows, to_lanes), 0.0).astype(BF16)
        mix_rows = dot_nt(to_rows, mix[...]).astype(BF16)
        mix_wide_t[...] = jnp.where(same, dot(mix_rows, to_lanes), 0.0).astype(BF16)
        bias_wide[...] = dot(bias[...], to_lanes.astype(F32), HIGHEST)
        for part in range(4):
            load(cot_hbm, cot, 4 + part, 4 * part).wait()

    def mix_forward():
        modes = gather_modes(0)
        spectrum[...] = modes
        doubled = dot_nt(modes.astype(BF16), in_wide[...])
        narrow2[...] = doubled
        for beta in range(RANK // 2):
            cols = slice(128 * beta, 128 * beta + 128)
            zed[:, cols] = (joined_wide[:, cols] * doubled).astype(BF16)
        scatter_modes(1, dot(zed[...], out_wide[...]))

    def activate(x, rows_x):
        rhs = jnp.concatenate([mix_wide[...], rows_x], axis=0)
        for y in range(0, NY, 128):
            lhs = jnp.concatenate([field[x, y : y + 128], second[y : y + 128, : 2 * MY]], axis=1)
            combined = dot(lhs, rhs) + bias_wide[...]
            cumulative = 0.5 + 0.5 * lax.erf(combined * math.sqrt(0.5))
            density = jnp.exp(-0.5 * combined * combined) * (1.0 / math.sqrt(2.0 * math.pi))
            act[x, y : y + 128] = (combined * cumulative).astype(BF16)
            derivative = cumulative + combined * density
            up[x, y : y + 128] = (cot[x, y : y + 128].astype(F32) * derivative).astype(BF16)

    def sweep(base, step):
        def body(j, carry):
            for s in range(2):
                x = 2 * j + s
                step(base + x, scratch[pl.ds(x, 2 * MY, stride=HALF), :].astype(BF16))
            return carry

        lax.fori_loop(0, HALF // 2, body, 0)

    def activation():
        total = jnp.zeros((1, FEATS), F32)
        for half in range(2):
            unpack(1, half)
            base = HALF * half
            sweep(base, activate)
            for x in range(0, HALF, 2):
                rows = analyse(up, base + x, x)
                total = total + rows[0:1, :FEATS] + rows[0:1, FEATS:]
            pack(2, half)
            send(2, half)
        rows_sum[...] = total

    def mix_gradient():
        products[...] = jnp.zeros_like(products)

        def accumulate(x, carry):
            products[...] += dot_tn(field[x], up[x])
            return carry

        lax.fori_loop(0, ROWS, accumulate, 0)

    def mix_backward():
        upstream = gather_modes(2)
        upstream_b = upstream.astype(BF16)
        dz = dot_nt(upstream_b, out_wide[...])
        dn = joined_wide[:, 0:128] * dz[:, 0:128]
        for beta in range(1, RANK // 2):
            cols = slice(128 * beta, 128 * beta + 128)
            dn = dn + joined_wide[:, cols] * dz[:, cols]
        dn_b = dn.astype(BF16)
        scatter_modes(3, dot(dn_b, in_wide[...]))
        return upstream_b, dz, dn_b

    def core_gradients(upstream_b, dz, dn_b):
        product = jnp.concatenate(
            [dz[:, 128 * b : 128 * b + 128] * narrow2[...] for b in range(RANK // 2)], axis=1
        ).astype(BF16)
        fold_rank = select((1024, RANK), lambda r, l: l == 2 * (r // 128) + (r % 128) // 64, BF16)
        djoined = dot(product, fold_rank)
        djoined = djoined[:MX] + djoined[MX:]
        place = select((MX, FEATS), lambda r, l: l == r + 32)
        first_part = dot(lax.dot_general(second_core[...], djoined, (((1,), (1,)), ((), ())), precision=HIGHEST), place, HIGHEST)
        unit = select((RANK, FEATS), lambda r, l: l == r)
        second_part = dot(dot(first_core[...], djoined, HIGHEST), unit, HIGHEST)
        packed = None
        for quarter in range(4):
            rows = []
            for beta in (2 * quarter, 2 * quarter + 1):
                outer = dot_tn(zed[:, 128 * beta : 128 * beta + 128], upstream_b)
                outer = jnp.where(in_keep, outer, 0.0)
                for base in (0, 64):
                    rows.append(
                        (outer[base : base + 16] + outer[base + 16 : base + 32])
                        + (outer[base + 32 : base + 48] + outer[base + 48 : base + 64])
                    )
            fold = select((FEATS, FEATS), lambda r, l, q=quarter: r % C + 32 * q == l, BF16)
            term = dot(jnp.concatenate(rows, axis=0).astype(BF16), fold)
            packed = term if packed is None else packed + term
        inner = jnp.where(in_keep, dot_tn(dn_b, spectrum[...].astype(BF16)), 0.0)
        inner = sum(inner[RANK * i : RANK * (i + 1)] for i in range(1, 2 * PLANES)) + inner[0:RANK]
        mixed = jnp.where(same, products[...], 0.0) * (MIX_SCALE / CORE_SCALE)
        mixed = (mixed[0:32] + mixed[32:64]) + (mixed[64:96] + mixed[96:128])
        stacked = jnp.concatenate([inner, mixed[:RANK], mixed[RANK:]], axis=1)
        fold = select(
            (3 * FEATS, FEATS), lambda r, l: r % C + jnp.where(r < FEATS, 0, 32 + 32 * (r // FEATS)) == l
        )
        misc = dot(stacked, fold, HIGHEST) + first_part
        unit = float(np.asarray(1.0 / math.sqrt(NY), dtype=np.float32).astype(jnp.bfloat16))
        bias_part = rows_sum[...] * (MIX_SCALE / CORE_SCALE / unit)
        for q in range(GROUPS):
            gsend[q, 0:8] = packed[8 * q : 8 * q + 8]
            gsend[q, 8:10] = misc[2 * q : 2 * q + 2]
            gsend[q, 10:11] = bias_part
            gsend[q, 11:16] = jnp.zeros((5, FEATS), F32)
            gsend[q, 16:32] = second_part

    def to_groups(source, target, sent, received):
        def start(i, carry):
            to = lax.rem(group + 1 + i, GROUPS)
            pltpu.make_async_remote_copy(
                src_ref=source(to), dst_ref=target.at[group], send_sem=sent, recv_sem=received,
                device_id={"dp": to}, device_id_type=MESH,
            ).start()
            return carry

        lax.fori_loop(0, GROUPS - 1, start, 0)

    def all_groups(target, sent, received):
        seven = target.at[pl.ds(0, GROUPS - 1)]
        return pltpu.make_async_remote_copy(
            src_ref=seven, dst_ref=seven, send_sem=sent, recv_sem=received,
            device_id={"dp": lax.rem(group + 1, GROUPS)}, device_id_type=MESH,
        )

    def all_pencils():
        others = brecv.at[pl.ds(0, PENCILS - 1)]
        return pltpu.make_async_remote_copy(
            src_ref=others, dst_ref=others, send_sem=bssem, recv_sem=brsem,
            device_id={"pencil": lax.rem(me + 1, PENCILS)}, device_id_type=MESH,
        )

    def sum_groups_send():
        to_groups(lambda to: gsend.at[to], grecv, gssem, grsem)
        grecv[group] = gsend[group]

    def sum_groups():
        all_groups(grecv, gssem, grsem).wait_recv()
        chunk = grecv[0]
        for q in range(1, GROUPS):
            chunk = chunk + grecv[q]
        second_out[...] = chunk[16:32] * CORE_SCALE
        bsend[...] = chunk[0:16].astype(BF16)

        def start(i, carry):
            to = lax.rem(me + 1 + i, PENCILS)
            pltpu.make_async_remote_copy(
                src_ref=bsend, dst_ref=brecv.at[me], send_sem=bssem, recv_sem=brsem,
                device_id={"pencil": to}, device_id_type=MESH,
            ).start()
            return carry

        lax.fori_loop(0, PENCILS - 1, start, 0)
        brecv[me] = bsend[...]

    def finish(x, rows_x):
        rhs = jnp.concatenate([mix_wide_t[...], rows_x], axis=0)
        for y in range(0, NY, 128):
            lhs = jnp.concatenate([up[x, y : y + 128], second[y : y + 128, : 2 * MY]], axis=1)
            adjoint[x, y : y + 128] = dot(lhs, rhs).astype(BF16)

    def finish_half(half):
        unpack(3, half)
        sweep(HALF * half, finish)

    def sum_pencils():
        all_pencils().wait_recv()
        total = brecv[0].astype(F32)
        for q in range(1, PENCILS):
            total = total + brecv[q].astype(F32)
        csend[...] = total * CORE_SCALE
        to_groups(lambda to: csend, grads_out, cssem, crsem)
        grads_out[group] = csend[...]

    def last():
        all_groups(grads_out, cssem, crsem).wait_recv()

    state = {}
    steps = [
        field_rows, weights, mix_forward, activation, mix_gradient,
        lambda: state.update(modes=mix_backward()),
        lambda: core_gradients(*state["modes"]),
        sum_groups_send, sum_groups, lambda: finish_half(0), lambda: finish_half(1), sum_pencils, last,
    ]
    for step in steps[:STOP]:
        step()

    if STOP > 12:
        all_groups(grads_out, cssem, crsem).wait_send()
    if STOP > 7:
        all_groups(grecv, gssem, grsem).wait_send()
    if STOP > 8:
        all_pencils().wait_send()
    for turn in range(4 if STOP > 5 else 3 if STOP > 3 else 2 if STOP > 2 else 1):
        for half in range(2):
            whole(turn, half).wait_send()


def write_out(
    act, adjoint, grads, second_in,
    act_hbm, adjoint_hbm, first_hbm, second_hbm, output_hbm, input_hbm, mix_hbm, bias_hbm,
    first, second, output, inner, mix, bias, sem,
):
    large = [
        pltpu.make_async_copy(act, act_hbm, sem.at[0]),
        pltpu.make_async_copy(adjoint, adjoint_hbm, sem.at[1]),
    ]
    for copy in large:
        copy.start()
    second[...] = second_in[:, :RANK]
    packed = grads[:, 0:8].reshape(64, FEATS)
    for quarter in range(4):
        output[64 * quarter : 64 * quarter + 64] = packed[:, 32 * quarter : 32 * quarter + 32]
    misc = jnp.concatenate([grads[q, 8:10] for q in range(GROUPS)], axis=0)
    inner[...] = misc[:, 0:32]
    first[...] = misc[:, 32:64]
    mix[0:RANK] = misc[:, 64:96]
    mix[RANK:C] = misc[:, 96:128]
    row = grads[0, 10:11]
    bias[...] = (row[:, 0:32] + row[:, 32:64]) + (row[:, 64:96] + row[:, 96:128])
    pairs = [
        (first, first_hbm), (second, second_hbm), (output, output_hbm),
        (inner, input_hbm), (mix, mix_hbm), (bias, bias_hbm),
    ]
    small = [pltpu.make_async_copy(a, b, sem.at[2 + i]) for i, (a, b) in enumerate(pairs)]
    for copy in small:
        copy.start()
    for copy in large + small:
        copy.wait()


def shards(field, cotangent, first_core, second_core, output_core, input_core, channel_mix, channel_bias):
    slab = (ROWS, NY, FEATS)
    vmem = pl.BlockSpec(memory_space=pltpu.VMEM)
    hbm = pl.BlockSpec(memory_space=pltpu.HBM)
    dma = pltpu.SemaphoreType.DMA
    smalls = [(RANK, MX), (RANK, RANK), (RANK * RANK, C), (RANK, C), (C, C), (1, C)]
    types = [F32, F32, F32, F32, BF16, F32]
    act, adjoint, grads, second_total = pl.pallas_call(
        kernel,
        out_shape=[
            jax.ShapeDtypeStruct(slab, BF16),
            jax.ShapeDtypeStruct(slab, BF16),
            jax.ShapeDtypeStruct((GROUPS, 16, FEATS), F32),
            jax.ShapeDtypeStruct((16, FEATS), F32),
        ],
        in_specs=[hbm] * 9,
        out_specs=[vmem] * 4,
        scratch_shapes=[
            pltpu.VMEM(slab, BF16),
            pltpu.VMEM(slab, BF16),
            pltpu.VMEM(slab, BF16),
            pltpu.VMEM((BLOCK, FEATS), F32),
            pltpu.VMEM((4, 2, PENCILS, MESSAGE, FEATS), BF16),
            pltpu.VMEM((4, 2, PENCILS, MESSAGE, FEATS), BF16),
        ]
        + [pltpu.VMEM(s, t) for s, t in zip(smalls, types)]
        + [
            pltpu.VMEM((2 * MY, NY), BF16),
            pltpu.VMEM((2 * MX, 2 * NX), BF16),
            pltpu.VMEM((NY, FEATS), BF16),
            pltpu.VMEM((2 * NX, FEATS), BF16),
            pltpu.VMEM((2 * MX, 1024), F32),
            pltpu.VMEM((1024, FEATS), BF16),
            pltpu.VMEM((FEATS, FEATS), BF16),
            pltpu.VMEM((FEATS, FEATS), BF16),
            pltpu.VMEM((FEATS, FEATS), BF16),
            pltpu.VMEM((1, FEATS), F32),
            pltpu.VMEM((2 * MX, FEATS), F32),
            pltpu.VMEM((2 * MX, 1024), BF16),
            pltpu.VMEM((2 * MX, FEATS), F32),
            pltpu.VMEM((FEATS, FEATS), F32),
            pltpu.VMEM((1, FEATS), F32),
            pltpu.VMEM((GROUPS, CHUNK, FEATS), F32),
            pltpu.VMEM((GROUPS, CHUNK, FEATS), F32),
            pltpu.VMEM((16, FEATS), BF16),
            pltpu.VMEM((PENCILS, 16, FEATS), BF16),
            pltpu.VMEM((16, FEATS), F32),
            dma((8,)),
            dma((20,)),
            dma((4, 2)),
            dma((4, 2)),
            dma,
            dma,
            dma,
            dma,
            dma,
            dma,
        ],
        compiler_params=pltpu.CompilerParams(
            collective_id=0, has_side_effects=True, vmem_limit_bytes=40 * 2**20
        ),
    )(
        *[
            pltpu.with_memory_space_constraint(a, pltpu.HBM)
            for a in (
                field[0],
                cotangent[0],
                first_core.T,
                second_core[:, 0, :],
                output_core.transpose(0, 2, 1).reshape(RANK * RANK, C),
                input_core,
                channel_mix,
                channel_bias[None],
                jnp.asarray(tables()),
            )
        ]
    )
    results = pl.pallas_call(
        write_out,
        out_shape=[jax.ShapeDtypeStruct(slab, BF16), jax.ShapeDtypeStruct(slab, BF16)]
        + [jax.ShapeDtypeStruct(s, F32) for s in smalls],
        in_specs=[vmem] * 4,
        out_specs=[hbm] * 8,
        scratch_shapes=[pltpu.VMEM(s, F32) for s in smalls] + [dma((8,))],
        compiler_params=pltpu.CompilerParams(vmem_limit_bytes=16 * 2**20),
    )(act, adjoint, grads, second_total)
    act, adjoint, first, second, output, inner, mix, bias = results
    return (
        act[None],
        adjoint[None],
        first.T,
        second[:, None, :],
        output.reshape(RANK, RANK, C).transpose(0, 2, 1),
        inner,
        mix,
        bias[0],
    )


def solution(mesh):
    slabs = P("dp", "pencil", None, None)
    column = P(None, "pencil", None)
    return jax.shard_map(
        shards,
        mesh=mesh,
        in_specs=(slabs, slabs, P(), column, P(), P(), P(), P()),
        out_specs=(slabs, slabs, P(), column, P(), P(), P(), P()),
        check_vma=False,
    )
```

time: 76.2 us -> 60.8 us (0.80)
  local copies, waits for them, and re-layouts: 17.4 us -> 0 us
  Pallas kernels: 57.7 us -> 60 us
    unnamed x26 -> x0, local copies, waits for them, and re-layouts: 15.2 us -> none
    pallas_call x0 -> x1, Pallas kernels: none -> 2.12 us  [shards(): pl.pallas_call(write_out, out_shape=[jax.ShapeDtypeStruct(slab, BF16), ja...]
    transpose x1 -> x0, local copies, waits for them, and re-layouts: 0.8 us -> none  [shards(): grads[:, 0:8].reshape(2, C, 8, RANK).transpose(0, 2, 1, 3)]
where the time goes in v2:
time: 60.8 us; the launch traced here: 60.6 us
  Pallas kernels  60 us (99%)
  between operations  0.64 us (1%)
    pallas_call x1, Pallas kernels, shards(): pl.pallas_call(kernel, out_shape=[jax.ShapeDtypeStruct(slab, BF16), jax.S...  57.9 us
    pallas_call x1, Pallas kernels, shards(): pl.pallas_call(write_out, out_shape=[jax.ShapeDtypeStruct(slab, BF16), ja...  2.12 us

profile of v2, /device:TPU:1, one launch (start us, length us, event | category | flops | bytes accessed | tf_op | source)
XLA Modules:
  0.0 60.6 jit_solution(17036287873464807080)
XLA Ops:
  0.6 57.9 %shard_map.152 = (bf16[16,512,128]{2,1,0:T(8,128)(2,1)S(1)}, bf16[16,512,128]{2,1,0:T(8,128)(2,1)S(1)}, f32[8,16,128]{2,1,0:T(8,128)S(1)}, f32[16,128]{1,0:T(8,128)S(1)}) custom-call(bf16[16,512,128]{2,1,0:T(8,128)(2,1)} %bitcast.18, bf16[16,512,128]{2,1,0:T(8,128)(2,1)} %bitcast.19, f32[16,32]{1,0:T(8,128)} %bitcast.21, f32[16,16]{1,0:T(8,128)} %bitcast.22, ...), custom_call_target="tpu_custom_call" | custom-call | tf_op jit(solution)/shard_map/pallas_call | solution.py:467
  58.5 2.1 %shard_map.153 = (bf16[16,512,128]{2,1,0:T(8,128)(2,1)}, bf16[16,512,128]{2,1,0:T(8,128)(2,1)}, f32[16,32]{1,0:T(8,128)}, f32[16,16]{1,0:T(8,128)}, f32[256,32]{...) custom-call(bf16[16,512,128]{2,1,0:T(8,128)(2,1)S(1)} %get-tuple-element.20.act, ...), custom_call_target="tpu_custom_call" | custom-call | tf_op jit(solution)/shard_map/pallas_call | solution.py:537

commit v3 on v2

--- a/solution.py
+++ b/solution.py
@@ -27,8 +27,10 @@
 HALF = ROWS // 2
 MESSAGE = 2 * HALF
 BLOCK = PENCILS * MESSAGE
-CHUNK = 32
-STOP = 13
+YS, ZS = 4, 8
+PARTS = GROUPS * YS
+CHUNK = 4
+STOP = 15
 CORE_SCALE = 1.0 / math.sqrt(GROUPS * PLANES * MX * MY)
 MIX_SCALE = 1.0 / math.sqrt(GROUPS * PLANES * NX * NY)
 
@@ -80,14 +82,16 @@
 def kernel(
     field_hbm, cot_hbm, first_hbm, second_hbm, output_hbm, input_hbm, mix_hbm, bias_hbm, table_hbm,
     act, adjoint, grads_out, second_out,
-    field, cot, up, scratch, sbuf, rbuf,
+    field, cot, up, scratch, analysed, sbuf, rbuf,
     first_core, second_core, output_core, input_core, mix, bias, second_t, first, second, first_t,
-    joined_wide, out_wide, in_wide, mix_wide, mix_wide_t, bias_wide, narrow2, zed, spectrum, products, rows_sum,
-    gsend, grecv, bsend, brecv, csend,
-    load_sem, small_sem, ssem, rsem, gssem, grsem, bssem, brsem, cssem, crsem,
+    joined_wide, out_wide, in_wide, mix_wide, mix_wide_t, bias_wide, narrow2, zed, spectrum, products, rows_sum, fold_rank, fold_lanes, misc,
+    gsend, grecv, bsend, brecv, csend, hsend, hrecv,
+    load_sem, small_sem, ssem, rsem, gssem, grsem, bssem, brsem, cssem, crsem, hssem, hrsem,
 ):
     me = lax.axis_index("pencil")
     group = lax.axis_index("dp")
+    z = lax.rem(me, ZS)
+    mine = group * YS + lax.div(me, ZS)
 
     def load(source, target, slot, x):
         return pltpu.make_async_copy(source.at[pl.ds(x, 4)], target.at[pl.ds(x, 4)], load_sem.at[slot])
@@ -110,17 +114,16 @@
     load(field_hbm, field, 0, 0).start()
     barrier = pltpu.get_barrier_semaphore()
 
-    def greet(i, carry):
-        pl.semaphore_signal(barrier, inc=1, device_id={"pencil": lax.rem(me + 1 + i, PENCILS)}, device_id_type=MESH)
-        return carry
-
-    lax.fori_loop(0, PENCILS - 1, greet, 0)
-
-    def greet_group(i, carry):
-        pl.semaphore_signal(barrier, inc=1, device_id={"dp": lax.rem(group + 1 + i, GROUPS)}, device_id_type=MESH)
-        return carry
-
-    lax.fori_loop(0, GROUPS - 1, greet_group, 0)
+    def wrap(i, size):
+        return jnp.where(i >= size, i - size, i)
+
+    column = me - z
+    greeted = [{"pencil": wrap(me + i, PENCILS)} for i in range(1, PENCILS)]
+    for i in range(1, GROUPS):
+        to = wrap(group + i, GROUPS)
+        greeted += [{"dp": to, "pencil": y * ZS + z} for y in range(YS)]
+    for to in greeted:
+        pl.semaphore_signal(barrier, inc=1, device_id=to, device_id_type=MESH)
     for part in range(1, 4):
         load(field_hbm, field, part, 4 * part).start()
     for copy in copies[4:]:
@@ -130,7 +133,7 @@
 
     def send(turn, half):
         def start(i, carry):
-            to = lax.rem(me + 1 + i, PENCILS)
+            to = wrap(me + 1 + i, PENCILS)
             pltpu.make_async_remote_copy(
                 src_ref=sbuf.at[turn, half, to],
                 dst_ref=rbuf.at[turn, half, me],
@@ -141,7 +144,7 @@
             ).start()
             return carry
 
-        lax.fori_loop(0, PENCILS - 1, start, 0)
+        lax.fori_loop(0, PENCILS - 1, start, 0, unroll=4)
         rbuf[turn, half, me] = sbuf[turn, half, me]
 
     def whole(turn, half):
@@ -157,12 +160,12 @@
     def analyse(source, x, x_half):
         pair = jnp.concatenate([source[x], source[x + 1]], axis=1)
         rows = dot(second_t[...], pair)
-        scratch[pl.ds(x_half, 2 * MY, stride=HALF), :] = rows[:, :FEATS]
-        scratch[pl.ds(x_half + 1, 2 * MY, stride=HALF), :] = rows[:, FEATS:]
+        analysed[pl.ds(x_half, 2 * MY, stride=HALF), :] = rows[:, :FEATS]
+        analysed[pl.ds(x_half + 1, 2 * MY, stride=HALF), :] = rows[:, FEATS:]
         return rows
 
     def pack(turn, half):
-        sbuf[turn, half] = scratch[...].astype(BF16).reshape(PENCILS, MESSAGE, FEATS)
+        sbuf[turn, half] = analysed[...].astype(BF16).reshape(PENCILS, MESSAGE, FEATS)
 
     def gather_modes(turn):
         total = None
@@ -196,8 +199,8 @@
                 for x in range(4 * part, 4 * part + 4, 2):
                     analyse(field, HALF * half + x, x)
             pack(0, half)
-            if half == 0:
-                pl.semaphore_wait(barrier, PENCILS + GROUPS - 2)
+        pl.semaphore_wait(barrier, len(greeted))
+        for half in range(2):
             send(0, half)
 
     def weights():
@@ -242,29 +245,33 @@
             lhs = jnp.concatenate([field[x, y : y + 128], second[y : y + 128, : 2 * MY]], axis=1)
             combined = dot(lhs, rhs) + bias_wide[...]
             cumulative = 0.5 + 0.5 * lax.erf(combined * math.sqrt(0.5))
-            density = jnp.exp(-0.5 * combined * combined) * (1.0 / math.sqrt(2.0 * math.pi))
+            density = jnp.exp2(combined * combined * (-0.5 * math.log2(math.e))) * (1.0 / math.sqrt(2.0 * math.pi))
             act[x, y : y + 128] = (combined * cumulative).astype(BF16)
             derivative = cumulative + combined * density
             up[x, y : y + 128] = (cot[x, y : y + 128].astype(F32) * derivative).astype(BF16)
 
     def sweep(base, step):
         def body(j, carry):
-            for s in range(2):
-                x = 2 * j + s
+            for i in range(4):
+                x = 4 * j + i
                 step(base + x, scratch[pl.ds(x, 2 * MY, stride=HALF), :].astype(BF16))
             return carry
 
-        lax.fori_loop(0, HALF // 2, body, 0)
+        lax.fori_loop(0, HALF // 4, body, 0)
 
     def activation():
         total = jnp.zeros((1, FEATS), F32)
         for half in range(2):
             unpack(1, half)
             base = HALF * half
+
+            def after(j, carry, base=base):
+                rows = analyse(up, base + 2 * j, 2 * j)
+                return carry + rows[0:1, :FEATS] + rows[0:1, FEATS:]
+
             sweep(base, activate)
-            for x in range(0, HALF, 2):
-                rows = analyse(up, base + x, x)
-                total = total + rows[0:1, :FEATS] + rows[0:1, FEATS:]
+            for j in range(HALF // 2):
+                total = after(j, total)
             pack(2, half)
             send(2, half)
         rows_sum[...] = total
@@ -286,100 +293,139 @@
         for beta in range(1, RANK // 2):
             cols = slice(128 * beta, 128 * beta + 128)
             dn = dn + joined_wide[:, cols] * dz[:, cols]
-        dn_b = dn.astype(BF16)
+        return upstream_b, dz, dn.astype(BF16)
+
+    def send_returned(upstream_b, dz, dn_b):
         scatter_modes(3, dot(dn_b, in_wide[...]))
-        return upstream_b, dz, dn_b
+
+    def fold_tables():
+        fold_rank[...] = select((1024, RANK), lambda r, l: l == 2 * (r // 128) + (r % 128) // 64, BF16)
+        fold_lanes[...] = select(
+            (4 * FEATS, FEATS), lambda r, l: r % C + 32 * (r // FEATS) == l, BF16
+        )
+        mixed = jnp.where(same, products[...], 0.0) * (MIX_SCALE / CORE_SCALE)
+        mixed = (mixed[0:32] + mixed[32:64]) + (mixed[64:96] + mixed[96:128])
+        unit = float(np.asarray(1.0 / math.sqrt(NY), dtype=np.float32).astype(jnp.bfloat16))
+        biases = rows_sum[...] * (MIX_SCALE / CORE_SCALE / unit)
+        fold = select((FEATS, FEATS), lambda r, l: r % C == l)
+        fold_bias = select((FEATS, FEATS), lambda r, l: r % C + 64 == l)
+        misc[...] = dot(mixed, fold, HIGHEST) + dot(biases, fold_bias, HIGHEST)
+        gsend[...] = jnp.zeros_like(gsend)
+        hsend[...] = jnp.zeros_like(hsend)
 
     def core_gradients(upstream_b, dz, dn_b):
         product = jnp.concatenate(
             [dz[:, 128 * b : 128 * b + 128] * narrow2[...] for b in range(RANK // 2)], axis=1
         ).astype(BF16)
-        fold_rank = select((1024, RANK), lambda r, l: l == 2 * (r // 128) + (r % 128) // 64, BF16)
-        djoined = dot(product, fold_rank)
-        djoined = djoined[:MX] + djoined[MX:]
-        place = select((MX, FEATS), lambda r, l: l == r + 32)
-        first_part = dot(lax.dot_general(second_core[...], djoined, (((1,), (1,)), ((), ())), precision=HIGHEST), place, HIGHEST)
-        unit = select((RANK, FEATS), lambda r, l: l == r)
-        second_part = dot(dot(first_core[...], djoined, HIGHEST), unit, HIGHEST)
-        packed = None
-        for quarter in range(4):
-            rows = []
-            for beta in (2 * quarter, 2 * quarter + 1):
-                outer = dot_tn(zed[:, 128 * beta : 128 * beta + 128], upstream_b)
-                outer = jnp.where(in_keep, outer, 0.0)
-                for base in (0, 64):
-                    rows.append(
-                        (outer[base : base + 16] + outer[base + 16 : base + 32])
-                        + (outer[base + 32 : base + 48] + outer[base + 48 : base + 64])
-                    )
-            fold = select((FEATS, FEATS), lambda r, l, q=quarter: r % C + 32 * q == l, BF16)
-            term = dot(jnp.concatenate(rows, axis=0).astype(BF16), fold)
-            packed = term if packed is None else packed + term
+        djoined = dot(product, fold_rank[...])
+        djoined = (djoined[:MX] + djoined[MX:]).astype(BF16)
+        first_part = dot_nt(second_core[...].astype(BF16), djoined)
+        second_part = dot(first_core[...].astype(BF16), djoined)
+        rows = []
+        for beta in range(RANK // 2):
+            outer = dot_tn(zed[:, 128 * beta : 128 * beta + 128], upstream_b)
+            outer = jnp.where(in_keep, outer, 0.0)
+            for base in (0, 64):
+                rows.append(
+                    (outer[base : base + 16] + outer[base + 16 : base + 32])
+                    + (outer[base + 32 : base + 48] + outer[base + 48 : base + 64])
+                )
+        wide = jnp.concatenate(
+            [jnp.concatenate(rows[4 * q : 4 * q + 4], axis=0) for q in range(4)], axis=1
+        )
+        packed = dot(wide.astype(BF16), fold_lanes[...])
         inner = jnp.where(in_keep, dot_tn(dn_b, spectrum[...].astype(BF16)), 0.0)
         inner = sum(inner[RANK * i : RANK * (i + 1)] for i in range(1, 2 * PLANES)) + inner[0:RANK]
-        mixed = jnp.where(same, products[...], 0.0) * (MIX_SCALE / CORE_SCALE)
-        mixed = (mixed[0:32] + mixed[32:64]) + (mixed[64:96] + mixed[96:128])
-        stacked = jnp.concatenate([inner, mixed[:RANK], mixed[RANK:]], axis=1)
-        fold = select(
-            (3 * FEATS, FEATS), lambda r, l: r % C + jnp.where(r < FEATS, 0, 32 + 32 * (r // FEATS)) == l
-        )
-        misc = dot(stacked, fold, HIGHEST) + first_part
-        unit = float(np.asarray(1.0 / math.sqrt(NY), dtype=np.float32).astype(jnp.bfloat16))
-        bias_part = rows_sum[...] * (MIX_SCALE / CORE_SCALE / unit)
-        for q in range(GROUPS):
-            gsend[q, 0:8] = packed[8 * q : 8 * q + 8]
-            gsend[q, 8:10] = misc[2 * q : 2 * q + 2]
-            gsend[q, 10:11] = bias_part
-            gsend[q, 11:16] = jnp.zeros((5, FEATS), F32)
-            gsend[q, 16:32] = second_part
-
-    def to_groups(source, target, sent, received):
+        inner = misc[0:RANK] + dot(inner.astype(BF16), fold_lanes[FEATS : 2 * FEATS])
+        for q in range(PARTS):
+            gsend[q, 0:2] = packed[2 * q : 2 * q + 2]
+        for q in range(RANK):
+            gsend[q, 2:3] = inner[q : q + 1]
+            gsend[RANK + q, 2:3] = misc[RANK + q : RANK + q + 1]
+            gsend[RANK + q, 2:3, 32:64] = first_part[q : q + 1]
+        hsend[:, 0:RANK] = second_part
+
+    def to_slice(source, target, sent, received):
         def start(i, carry):
-            to = lax.rem(group + 1 + i, GROUPS)
+            other = wrap(group + i, GROUPS)
+            for y in range(YS):
+                to = other * YS + y
+                pltpu.make_async_remote_copy(
+                    src_ref=source(to), dst_ref=target.at[mine], send_sem=sent, recv_sem=received,
+                    device_id={"dp": other, "pencil": y * ZS + z}, device_id_type=MESH,
+                ).start()
+            return carry
+
+        lax.fori_loop(1, GROUPS, start, 0)
+        for i in range(1, YS):
+            pencil = wrap(me + i * ZS, PENCILS)
+            to = wrap(mine - group * YS + i, YS) + group * YS
             pltpu.make_async_remote_copy(
-                src_ref=source(to), dst_ref=target.at[group], send_sem=sent, recv_sem=received,
-                device_id={"dp": to}, device_id_type=MESH,
+                src_ref=source(to), dst_ref=target.at[mine], send_sem=sent, recv_sem=received,
+                device_id={"pencil": pencil}, device_id_type=MESH,
             ).start()
-            return carry
-
-        lax.fori_loop(0, GROUPS - 1, start, 0)
-
-    def all_groups(target, sent, received):
-        seven = target.at[pl.ds(0, GROUPS - 1)]
+
+    def wait_for(target, count, sent, received):
+        others = target.at[pl.ds(0, count)]
         return pltpu.make_async_remote_copy(
-            src_ref=seven, dst_ref=seven, send_sem=sent, recv_sem=received,
-            device_id={"dp": lax.rem(group + 1, GROUPS)}, device_id_type=MESH,
-        )
-
-    def all_pencils():
-        others = brecv.at[pl.ds(0, PENCILS - 1)]
-        return pltpu.make_async_remote_copy(
-            src_ref=others, dst_ref=others, send_sem=bssem, recv_sem=brsem,
+            src_ref=others, dst_ref=others, send_sem=sent, recv_sem=received,
             device_id={"pencil": lax.rem(me + 1, PENCILS)}, device_id_type=MESH,
         )
 
-    def sum_groups_send():
-        to_groups(lambda to: gsend.at[to], grecv, gssem, grsem)
-        grecv[group] = gsend[group]
-
-    def sum_groups():
-        all_groups(grecv, gssem, grsem).wait_recv()
+    all_slice = wait_for(grecv, PARTS - 1, gssem, grsem)
+    all_column = wait_for(brecv, ZS - 1, bssem, brsem)
+    all_last = wait_for(grads_out, PARTS - 1, cssem, crsem)
+    all_seconds = wait_for(hrecv, GROUPS - 1, hssem, hrsem)
+
+    def sum_slice_send():
+        to_slice(lambda to: gsend.at[to], grecv, gssem, grsem)
+        grecv[mine] = gsend[mine]
+
+    def sum_slice():
+        all_slice.wait_recv()
         chunk = grecv[0]
-        for q in range(1, GROUPS):
+        for q in range(1, PARTS):
             chunk = chunk + grecv[q]
-        second_out[...] = chunk[16:32] * CORE_SCALE
-        bsend[...] = chunk[0:16].astype(BF16)
+        bsend[...] = chunk
 
         def start(i, carry):
-            to = lax.rem(me + 1 + i, PENCILS)
+            to = column + wrap(z + 1 + i, ZS)
             pltpu.make_async_remote_copy(
-                src_ref=bsend, dst_ref=brecv.at[me], send_sem=bssem, recv_sem=brsem,
+                src_ref=bsend, dst_ref=brecv.at[z], send_sem=bssem, recv_sem=brsem,
                 device_id={"pencil": to}, device_id_type=MESH,
             ).start()
             return carry
 
-        lax.fori_loop(0, PENCILS - 1, start, 0)
-        brecv[me] = bsend[...]
+        lax.fori_loop(0, ZS - 1, start, 0)
+        brecv[z] = chunk
+
+        def start_second(i, carry):
+            pltpu.make_async_remote_copy(
+                src_ref=hsend, dst_ref=hrecv.at[group], send_sem=hssem, recv_sem=hrsem,
+                device_id={"dp": wrap(group + 1 + i, GROUPS)}, device_id_type=MESH,
+            ).start()
+            return carry
+
+        lax.fori_loop(0, GROUPS - 1, start_second, 0)
+        hrecv[group] = hsend[...]
+
+    def sum_column():
+        all_column.wait_recv()
+        total = brecv[0]
+        for q in range(1, ZS):
+            total = total + brecv[q]
+        total = total * CORE_SCALE
+        csend[...] = total
+        to_slice(lambda to: csend, grads_out, cssem, crsem)
+        grads_out[mine] = total
+
+    def last():
+        all_seconds.wait_recv()
+        total = hrecv[0]
+        for q in range(1, GROUPS):
+            total = total + hrecv[q]
+        second_out[...] = total * CORE_SCALE
+        all_last.wait_recv()
 
     def finish(x, rows_x):
         rhs = jnp.concatenate([mix_wide_t[...], rows_x], axis=0)
@@ -391,35 +437,20 @@
         unpack(3, half)
         sweep(HALF * half, finish)
 
-    def sum_pencils():
-        all_pencils().wait_recv()
-        total = brecv[0].astype(F32)
-        for q in range(1, PENCILS):
-            total = total + brecv[q].astype(F32)
-        csend[...] = total * CORE_SCALE
-        to_groups(lambda to: csend, grads_out, cssem, crsem)
-        grads_out[group] = csend[...]
-
-    def last():
-        all_groups(grads_out, cssem, crsem).wait_recv()
-
     state = {}
     steps = [
-        field_rows, weights, mix_forward, activation, mix_gradient,
+        field_rows, weights, mix_forward, activation, mix_gradient, fold_tables,
         lambda: state.update(modes=mix_backward()),
         lambda: core_gradients(*state["modes"]),
-        sum_groups_send, sum_groups, lambda: finish_half(0), lambda: finish_half(1), sum_pencils, last,
+        sum_slice_send, lambda: send_returned(*state["modes"]),
+        sum_slice, lambda: finish_half(0), sum_column, lambda: finish_half(1), last,
     ]
     for step in steps[:STOP]:
         step()
 
-    if STOP > 12:
-        all_groups(grads_out, cssem, crsem).wait_send()
-    if STOP > 7:
-        all_groups(grecv, gssem, grsem).wait_send()
-    if STOP > 8:
-        all_pencils().wait_send()
-    for turn in range(4 if STOP > 5 else 3 if STOP > 3 else 2 if STOP > 2 else 1):
+    for copy in (all_slice, all_column, all_last, all_seconds):
+        copy.wait_send()
+    for turn in range(4):
         for half in range(2):
             whole(turn, half).wait_send()
 
@@ -427,30 +458,30 @@
 def write_out(
     act, adjoint, grads, second_in,
     act_hbm, adjoint_hbm, first_hbm, second_hbm, output_hbm, input_hbm, mix_hbm, bias_hbm,
-    first, second, output, inner, mix, bias, sem,
+    first, second, output, inner, mix, bias, packed, misc, sem,
 ):
-    large = [
-        pltpu.make_async_copy(act, act_hbm, sem.at[0]),
-        pltpu.make_async_copy(adjoint, adjoint_hbm, sem.at[1]),
-    ]
+    large = []
+    for i in range(4):
+        part = pl.ds(ROWS // 4 * i, ROWS // 4)
+        large.append(pltpu.make_async_copy(act.at[part], act_hbm.at[part], sem.at[6 + i]))
+        large.append(pltpu.make_async_copy(adjoint.at[part], adjoint_hbm.at[part], sem.at[10 + i]))
     for copy in large:
         copy.start()
     second[...] = second_in[:, :RANK]
-    packed = grads[:, 0:8].reshape(64, FEATS)
+    for q in range(PARTS):
+        packed[2 * q : 2 * q + 2] = grads[q, 0:2]
+        misc[q : q + 1] = grads[q, 2:3]
     for quarter in range(4):
         output[64 * quarter : 64 * quarter + 64] = packed[:, 32 * quarter : 32 * quarter + 32]
-    misc = jnp.concatenate([grads[q, 8:10] for q in range(GROUPS)], axis=0)
-    inner[...] = misc[:, 0:32]
-    first[...] = misc[:, 32:64]
-    mix[0:RANK] = misc[:, 64:96]
-    mix[RANK:C] = misc[:, 96:128]
-    row = grads[0, 10:11]
-    bias[...] = (row[:, 0:32] + row[:, 32:64]) + (row[:, 64:96] + row[:, 96:128])
+    mix[...] = misc[:, 0:32]
+    inner[...] = misc[0:RANK, 32:64]
+    first[...] = misc[RANK:C, 32:64]
+    bias[...] = misc[0:1, 64:96]
     pairs = [
         (first, first_hbm), (second, second_hbm), (output, output_hbm),
         (inner, input_hbm), (mix, mix_hbm), (bias, bias_hbm),
     ]
-    small = [pltpu.make_async_copy(a, b, sem.at[2 + i]) for i, (a, b) in enumerate(pairs)]
+    small = [pltpu.make_async_copy(a, b, sem.at[i]) for i, (a, b) in enumerate(pairs)]
     for copy in small:
         copy.start()
     for copy in large + small:
@@ -469,7 +500,7 @@
         out_shape=[
             jax.ShapeDtypeStruct(slab, BF16),
             jax.ShapeDtypeStruct(slab, BF16),
-            jax.ShapeDtypeStruct((GROUPS, 16, FEATS), F32),
+            jax.ShapeDtypeStruct((PARTS, CHUNK, FEATS), F32),
             jax.ShapeDtypeStruct((16, FEATS), F32),
         ],
         in_specs=[hbm] * 9,
@@ -478,6 +509,7 @@
             pltpu.VMEM(slab, BF16),
             pltpu.VMEM(slab, BF16),
             pltpu.VMEM(slab, BF16),
+            pltpu.VMEM((BLOCK, FEATS), F32),
             pltpu.VMEM((BLOCK, FEATS), F32),
             pltpu.VMEM((4, 2, PENCILS, MESSAGE, FEATS), BF16),
             pltpu.VMEM((4, 2, PENCILS, MESSAGE, FEATS), BF16),
@@ -499,15 +531,22 @@
             pltpu.VMEM((2 * MX, FEATS), F32),
             pltpu.VMEM((FEATS, FEATS), F32),
             pltpu.VMEM((1, FEATS), F32),
-            pltpu.VMEM((GROUPS, CHUNK, FEATS), F32),
-            pltpu.VMEM((GROUPS, CHUNK, FEATS), F32),
-            pltpu.VMEM((16, FEATS), BF16),
-            pltpu.VMEM((PENCILS, 16, FEATS), BF16),
-            pltpu.VMEM((16, FEATS), F32),
+            pltpu.VMEM((1024, RANK), BF16),
+            pltpu.VMEM((4 * FEATS, FEATS), BF16),
+            pltpu.VMEM((C, FEATS), F32),
+            pltpu.VMEM((PARTS, CHUNK, FEATS), F32),
+            pltpu.VMEM((PARTS, CHUNK, FEATS), F32),
+            pltpu.VMEM((CHUNK, FEATS), F32),
+            pltpu.VMEM((ZS, CHUNK, FEATS), F32),
+            pltpu.VMEM((CHUNK, FEATS), F32),
+            pltpu.VMEM((RANK, FEATS), F32),
+            pltpu.VMEM((GROUPS, RANK, FEATS), F32),
             dma((8,)),
             dma((20,)),
             dma((4, 2)),
             dma((4, 2)),
+            dma,
+            dma,
             dma,
             dma,
             dma,
@@ -540,7 +579,7 @@
         + [jax.ShapeDtypeStruct(s, F32) for s in smalls],
         in_specs=[vmem] * 4,
         out_specs=[hbm] * 8,
-        scratch_shapes=[pltpu.VMEM(s, F32) for s in smalls] + [dma((8,))],
+        scratch_shapes=[pltpu.VMEM(s, F32) for s in smalls + [(64, FEATS), (C, FEATS)]] + [dma((14,))],
         compiler_params=pltpu.CompilerParams(vmem_limit_bytes=16 * 2**20),
     )(act, adjoint, grads, second_total)
     act, adjoint, first, second, output, inner, mix, bias = results

time: 60.8 us -> 58.3 us (0.959)
  Pallas kernels: 60 us -> 57.5 us
    pallas_call x1, Pallas kernels: 57.9 us -> 55.3 us  [shards(): pl.pallas_call(kernel, out_shape=[jax.ShapeDtypeStruct(slab, BF16), jax.S...]
where the time goes in v3:
time: 58.3 us; the launch traced here: 58.1 us
  Pallas kernels  57.5 us (99%)
  between operations  0.64 us (1%)
    pallas_call x1, Pallas kernels, shards(): pl.pallas_call(kernel, out_shape=[jax.ShapeDtypeStruct(slab, BF16), jax.S...  55.3 us
    pallas_call x1, Pallas kernels, shards(): pl.pallas_call(write_out, out_shape=[jax.ShapeDtypeStruct(slab, BF16), ja...  2.2 us

profile of v3, /device:TPU:1, one launch (start us, length us, event | category | flops | bytes accessed | tf_op | source)
XLA Modules:
  0.0 58.1 jit_solution(4167590112954882882)
XLA Ops:
  0.6 55.3 %shard_map.152 = (bf16[16,512,128]{2,1,0:T(8,128)(2,1)S(1)}, bf16[16,512,128]{2,1,0:T(8,128)(2,1)S(1)}, f32[32,4,128]{2,1,0:T(4,128)S(1)}, f32[16,128]{1,0:T(8,128)S(1)}) custom-call(bf16[16,512,128]{2,1,0:T(8,128)(2,1)} %bitcast.18, bf16[16,512,128]{2,1,0:T(8,128)(2,1)} %bitcast.19, f32[16,32]{1,0:T(8,128)} %bitcast.21, f32[16,16]{1,0:T(8,128)} %bitcast.22, ...), custom_call_target="tpu_custom_call" | custom-call | tf_op jit(solution)/shard_map/pallas_call | solution.py:498
  55.9 2.2 %shard_map.153 = (bf16[16,512,128]{2,1,0:T(8,128)(2,1)}, bf16[16,512,128]{2,1,0:T(8,128)(2,1)}, f32[16,32]{1,0:T(8,128)}, f32[16,16]{1,0:T(8,128)}, f32[256,32]{...) custom-call(bf16[16,512,128]{2,1,0:T(8,128)(2,1)S(1)} %get-tuple-element.20.act, ...), custom_call_target="tpu_custom_call" | custom-call | tf_op jit(solution)/shard_map/pallas_call | solution.py:576

commit v4 on v3

--- a/solution.py
+++ b/solution.py
@@ -27,10 +27,11 @@
 HALF = ROWS // 2
 MESSAGE = 2 * HALF
 BLOCK = PENCILS * MESSAGE
-YS, ZS = 4, 8
-PARTS = GROUPS * YS
-CHUNK = 4
-STOP = 15
+CHUNK = 16
+FARTHEST = sorted(
+    [(y, z) for y in range(4) for z in range(8) if y + z],
+    key=lambda step: (-min(step[0], 4 - step[0]) - min(step[1], 8 - step[1]), step),
+)
 CORE_SCALE = 1.0 / math.sqrt(GROUPS * PLANES * MX * MY)
 MIX_SCALE = 1.0 / math.sqrt(GROUPS * PLANES * NX * NY)
 
@@ -85,13 +86,13 @@
     field, cot, up, scratch, analysed, sbuf, rbuf,
     first_core, second_core, output_core, input_core, mix, bias, second_t, first, second, first_t,
     joined_wide, out_wide, in_wide, mix_wide, mix_wide_t, bias_wide, narrow2, zed, spectrum, products, rows_sum, fold_rank, fold_lanes, misc,
-    gsend, grecv, bsend, brecv, csend, hsend, hrecv,
-    load_sem, small_sem, ssem, rsem, gssem, grsem, bssem, brsem, cssem, crsem, hssem, hrsem,
+    rest, gsend, grecv, bsend, brecv, csend,
+    load_sem, small_sem, ssem, rsem, gssem, grsem, bssem, brsem, cssem, crsem,
 ):
     me = lax.axis_index("pencil")
     group = lax.axis_index("dp")
-    z = lax.rem(me, ZS)
-    mine = group * YS + lax.div(me, ZS)
+    spot = lax.rem(me, 8)
+    row = me - spot
 
     def load(source, target, slot, x):
         return pltpu.make_async_copy(source.at[pl.ds(x, 4)], target.at[pl.ds(x, 4)], load_sem.at[slot])
@@ -117,11 +118,8 @@
     def wrap(i, size):
         return jnp.where(i >= size, i - size, i)
 
-    column = me - z
     greeted = [{"pencil": wrap(me + i, PENCILS)} for i in range(1, PENCILS)]
-    for i in range(1, GROUPS):
-        to = wrap(group + i, GROUPS)
-        greeted += [{"dp": to, "pencil": y * ZS + z} for y in range(YS)]
+    greeted += [{"dp": wrap(group + i, GROUPS)} for i in range(1, GROUPS)]
     for to in greeted:
         pl.semaphore_signal(barrier, inc=1, device_id=to, device_id_type=MESH)
     for part in range(1, 4):
@@ -132,8 +130,8 @@
         load(cot_hbm, cot, 4 + part, 4 * part).start()
 
     def send(turn, half):
-        def start(i, carry):
-            to = wrap(me + 1 + i, PENCILS)
+        for dy, dz in FARTHEST:
+            to = wrap(row + dy * 8, PENCILS) + wrap(spot + dz, 8)
             pltpu.make_async_remote_copy(
                 src_ref=sbuf.at[turn, half, to],
                 dst_ref=rbuf.at[turn, half, me],
@@ -142,9 +140,6 @@
                 device_id={"pencil": to},
                 device_id_type=MESH,
             ).start()
-            return carry
-
-        lax.fori_loop(0, PENCILS - 1, start, 0, unroll=4)
         rbuf[turn, half, me] = sbuf[turn, half, me]
 
     def whole(turn, half):
@@ -299,7 +294,9 @@
         scatter_modes(3, dot(dn_b, in_wide[...]))
 
     def fold_tables():
-        fold_rank[...] = select((1024, RANK), lambda r, l: l == 2 * (r // 128) + (r % 128) // 64, BF16)
+        fold_rank[...] = select(
+            (1024, FEATS), lambda r, l: l % RANK == 2 * (r // 128) + (r % 128) // 64, BF16
+        )
         fold_lanes[...] = select(
             (4 * FEATS, FEATS), lambda r, l: r % C + 32 * (r // FEATS) == l, BF16
         )
@@ -310,8 +307,6 @@
         fold = select((FEATS, FEATS), lambda r, l: r % C == l)
         fold_bias = select((FEATS, FEATS), lambda r, l: r % C + 64 == l)
         misc[...] = dot(mixed, fold, HIGHEST) + dot(biases, fold_bias, HIGHEST)
-        gsend[...] = jnp.zeros_like(gsend)
-        hsend[...] = jnp.zeros_like(hsend)
 
     def core_gradients(upstream_b, dz, dn_b):
         product = jnp.concatenate(
@@ -319,8 +314,13 @@
         ).astype(BF16)
         djoined = dot(product, fold_rank[...])
         djoined = (djoined[:MX] + djoined[MX:]).astype(BF16)
-        first_part = dot_nt(second_core[...].astype(BF16), djoined)
+        first_part = dot_nt(second_core[...].astype(BF16), djoined[:, :RANK])
         second_part = dot(first_core[...].astype(BF16), djoined)
+        rows16, lanes16 = iotas((RANK, FEATS))
+        second_part = jnp.where(rows16 % 8 == lanes16 // RANK, second_part, 0.0)
+        second_part = jnp.concatenate(
+            [jnp.sum(second_part[8 * i : 8 * i + 8], axis=0, keepdims=True) for i in range(2)], axis=0
+        )
         rows = []
         for beta in range(RANK // 2):
             outer = dot_tn(zed[:, 128 * beta : 128 * beta + 128], upstream_b)
@@ -337,33 +337,23 @@
         inner = jnp.where(in_keep, dot_tn(dn_b, spectrum[...].astype(BF16)), 0.0)
         inner = sum(inner[RANK * i : RANK * (i + 1)] for i in range(1, 2 * PLANES)) + inner[0:RANK]
         inner = misc[0:RANK] + dot(inner.astype(BF16), fold_lanes[FEATS : 2 * FEATS])
-        for q in range(PARTS):
-            gsend[q, 0:2] = packed[2 * q : 2 * q + 2]
-        for q in range(RANK):
-            gsend[q, 2:3] = inner[q : q + 1]
-            gsend[RANK + q, 2:3] = misc[RANK + q : RANK + q + 1]
-            gsend[RANK + q, 2:3, 32:64] = first_part[q : q + 1]
-        hsend[:, 0:RANK] = second_part
-
-    def to_slice(source, target, sent, received):
+        rest[...] = misc[...]
+        rest[0:RANK] = inner
+        rest[RANK:C, 32:64] = first_part
+        for q in range(GROUPS):
+            parts = [packed[8 * q : 8 * q + 8], rest[4 * q : 4 * q + 4], second_part, jnp.zeros((2, FEATS), F32)]
+            gsend[q] = jnp.concatenate(parts, axis=0).astype(BF16)
+
+    def to_groups(source, target, sent, received):
         def start(i, carry):
-            other = wrap(group + i, GROUPS)
-            for y in range(YS):
-                to = other * YS + y
-                pltpu.make_async_remote_copy(
-                    src_ref=source(to), dst_ref=target.at[mine], send_sem=sent, recv_sem=received,
-                    device_id={"dp": other, "pencil": y * ZS + z}, device_id_type=MESH,
-                ).start()
+            to = wrap(group + i, GROUPS)
+            pltpu.make_async_remote_copy(
+                src_ref=source(to), dst_ref=target.at[group], send_sem=sent, recv_sem=received,
+                device_id={"dp": to}, device_id_type=MESH,
+            ).start()
             return carry
 
-        lax.fori_loop(1, GROUPS, start, 0)
-        for i in range(1, YS):
-            pencil = wrap(me + i * ZS, PENCILS)
-            to = wrap(mine - group * YS + i, YS) + group * YS
-            pltpu.make_async_remote_copy(
-                src_ref=source(to), dst_ref=target.at[mine], send_sem=sent, recv_sem=received,
-                device_id={"pencil": pencil}, device_id_type=MESH,
-            ).start()
+        lax.fori_loop(1, GROUPS, start, 0, unroll=True)
 
     def wait_for(target, count, sent, received):
         others = target.at[pl.ds(0, count)]
@@ -372,59 +362,43 @@
             device_id={"pencil": lax.rem(me + 1, PENCILS)}, device_id_type=MESH,
         )
 
-    all_slice = wait_for(grecv, PARTS - 1, gssem, grsem)
-    all_column = wait_for(brecv, ZS - 1, bssem, brsem)
-    all_last = wait_for(grads_out, PARTS - 1, cssem, crsem)
-    all_seconds = wait_for(hrecv, GROUPS - 1, hssem, hrsem)
-
-    def sum_slice_send():
-        to_slice(lambda to: gsend.at[to], grecv, gssem, grsem)
-        grecv[mine] = gsend[mine]
-
-    def sum_slice():
-        all_slice.wait_recv()
-        chunk = grecv[0]
-        for q in range(1, PARTS):
-            chunk = chunk + grecv[q]
-        bsend[...] = chunk
+    all_groups = wait_for(grecv, GROUPS - 1, gssem, grsem)
+    all_pencils = wait_for(brecv, PENCILS - 1, bssem, brsem)
+    all_last = wait_for(grads_out, GROUPS - 1, cssem, crsem)
+
+    def sum_groups_send():
+        to_groups(lambda to: gsend.at[to], grecv, gssem, grsem)
+        grecv[group] = gsend[group]
+
+    def sum_groups():
+        all_groups.wait_recv()
+        chunk = grecv[0].astype(F32)
+        for q in range(1, GROUPS):
+            chunk = chunk + grecv[q].astype(F32)
+        second_out[...] = chunk * CORE_SCALE
+        bsend[...] = chunk.astype(BF16)
 
         def start(i, carry):
-            to = column + wrap(z + 1 + i, ZS)
             pltpu.make_async_remote_copy(
-                src_ref=bsend, dst_ref=brecv.at[z], send_sem=bssem, recv_sem=brsem,
-                device_id={"pencil": to}, device_id_type=MESH,
+                src_ref=bsend, dst_ref=brecv.at[me], send_sem=bssem, recv_sem=brsem,
+                device_id={"pencil": wrap(me + 1 + i, PENCILS)}, device_id_type=MESH,
             ).start()
             return carry
 
-        lax.fori_loop(0, ZS - 1, start, 0)
-        brecv[z] = chunk
-
-        def start_second(i, carry):
-            pltpu.make_async_remote_copy(
-                src_ref=hsend, dst_ref=hrecv.at[group], send_sem=hssem, recv_sem=hrsem,
-                device_id={"dp": wrap(group + 1 + i, GROUPS)}, device_id_type=MESH,
-            ).start()
-            return carry
-
-        lax.fori_loop(0, GROUPS - 1, start_second, 0)
-        hrecv[group] = hsend[...]
-
-    def sum_column():
-        all_column.wait_recv()
-        total = brecv[0]
-        for q in range(1, ZS):
-            total = total + brecv[q]
+        lax.fori_loop(0, PENCILS - 1, start, 0, unroll=4)
+        brecv[me] = bsend[...]
+
+    def sum_pencils():
+        all_pencils.wait_recv()
+        total = brecv[0].astype(F32)
+        for q in range(1, PENCILS):
+            total = total + brecv[q].astype(F32)
         total = total * CORE_SCALE
         csend[...] = total
-        to_slice(lambda to: csend, grads_out, cssem, crsem)
-        grads_out[mine] = total
+        to_groups(lambda to: csend, grads_out, cssem, crsem)
+        grads_out[group] = total
 
     def last():
-        all_seconds.wait_recv()
-        total = hrecv[0]
-        for q in range(1, GROUPS):
-            total = total + hrecv[q]
-        second_out[...] = total * CORE_SCALE
         all_last.wait_recv()
 
     def finish(x, rows_x):
@@ -442,13 +416,13 @@
         field_rows, weights, mix_forward, activation, mix_gradient, fold_tables,
         lambda: state.update(modes=mix_backward()),
         lambda: core_gradients(*state["modes"]),
-        sum_slice_send, lambda: send_returned(*state["modes"]),
-        sum_slice, lambda: finish_half(0), sum_column, lambda: finish_half(1), last,
+        sum_groups_send, lambda: send_returned(*state["modes"]),
+        sum_groups, lambda: finish_half(0), sum_pencils, lambda: finish_half(1), last,
     ]
-    for step in steps[:STOP]:
+    for step in steps:
         step()
 
-    for copy in (all_slice, all_column, all_last, all_seconds):
+    for copy in (all_groups, all_pencils, all_last):
         copy.wait_send()
     for turn in range(4):
         for half in range(2):
@@ -467,10 +441,11 @@
         large.append(pltpu.make_async_copy(adjoint.at[part], adjoint_hbm.at[part], sem.at[10 + i]))
     for copy in large:
         copy.start()
-    second[...] = second_in[:, :RANK]
-    for q in range(PARTS):
-        packed[2 * q : 2 * q + 2] = grads[q, 0:2]
-        misc[q : q + 1] = grads[q, 2:3]
+    for i in range(RANK):
+        second[i : i + 1] = second_in[12 + i // 8 : 13 + i // 8, RANK * (i % 8) : RANK * (i % 8) + RANK]
+    for q in range(GROUPS):
+        packed[8 * q : 8 * q + 8] = grads[q, 0:8]
+        misc[4 * q : 4 * q + 4] = grads[q, 8:12]
     for quarter in range(4):
         output[64 * quarter : 64 * quarter + 64] = packed[:, 32 * quarter : 32 * quarter + 32]
     mix[...] = misc[:, 0:32]
@@ -500,7 +475,7 @@
         out_shape=[
             jax.ShapeDtypeStruct(slab, BF16),
             jax.ShapeDtypeStruct(slab, BF16),
-            jax.ShapeDtypeStruct((PARTS, CHUNK, FEATS), F32),
+            jax.ShapeDtypeStruct((GROUPS, CHUNK, FEATS), F32),
             jax.ShapeDtypeStruct((16, FEATS), F32),
         ],
         in_specs=[hbm] * 9,
@@ -531,22 +506,19 @@
             pltpu.VMEM((2 * MX, FEATS), F32),
             pltpu.VMEM((FEATS, FEATS), F32),
             pltpu.VMEM((1, FEATS), F32),
-            pltpu.VMEM((1024, RANK), BF16),
+            pltpu.VMEM((1024, FEATS), BF16),
             pltpu.VMEM((4 * FEATS, FEATS), BF16),
             pltpu.VMEM((C, FEATS), F32),
-            pltpu.VMEM((PARTS, CHUNK, FEATS), F32),
-            pltpu.VMEM((PARTS, CHUNK, FEATS), F32),
+            pltpu.VMEM((C, FEATS), F32),
+            pltpu.VMEM((GROUPS, CHUNK, FEATS), BF16),
+            pltpu.VMEM((GROUPS, CHUNK, FEATS), BF16),
+            pltpu.VMEM((CHUNK, FEATS), BF16),
+            pltpu.VMEM((PENCILS, CHUNK, FEATS), BF16),
             pltpu.VMEM((CHUNK, FEATS), F32),
-            pltpu.VMEM((ZS, CHUNK, FEATS), F32),
-            pltpu.VMEM((CHUNK, FEATS), F32),
-            pltpu.VMEM((RANK, FEATS), F32),
-            pltpu.VMEM((GROUPS, RANK, FEATS), F32),
             dma((8,)),
             dma((20,)),
             dma((4, 2)),
             dma((4, 2)),
-            dma,
-            dma,
             dma,
             dma,
             dma,

time: 58.3 us -> 55.4 us (0.950)
  Pallas kernels: 57.5 us -> 54.6 us
    pallas_call x1, Pallas kernels: 55.3 us -> 52.4 us  [shards(): pl.pallas_call(kernel, out_shape=[jax.ShapeDtypeStruct(slab, BF16), jax.S...]
where the time goes in v4:
time: 55.4 us; the launch traced here: 55.2 us
  Pallas kernels  54.6 us (99%)
  between operations  0.64 us (1%)
    pallas_call x1, Pallas kernels, shards(): pl.pallas_call(kernel, out_shape=[jax.ShapeDtypeStruct(slab, BF16), jax.S...  52.4 us
    pallas_call x1, Pallas kernels, shards(): pl.pallas_call(write_out, out_shape=[jax.ShapeDtypeStruct(slab, BF16), ja...  2.19 us

profile of v4, /device:TPU:1, one launch (start us, length us, event | category | flops | bytes accessed | tf_op | source)
XLA Modules:
  0.0 55.2 jit_solution(14218540019800178815)
XLA Ops:
  0.6 52.4 %shard_map.152 = (bf16[16,512,128]{2,1,0:T(8,128)(2,1)S(1)}, bf16[16,512,128]{2,1,0:T(8,128)(2,1)S(1)}, f32[8,16,128]{2,1,0:T(8,128)S(1)}, f32[16,128]{1,0:T(8,128)S(1)}) custom-call(bf16[16,512,128]{2,1,0:T(8,128)(2,1)} %bitcast.18, bf16[16,512,128]{2,1,0:T(8,128)(2,1)} %bitcast.19, f32[16,32]{1,0:T(8,128)} %bitcast.21, f32[16,16]{1,0:T(8,128)} %bitcast.22, ...), custom_call_target="tpu_custom_call" | custom-call | tf_op jit(solution)/shard_map/pallas_call | solution.py:473
  53.0 2.2 %shard_map.153 = (bf16[16,512,128]{2,1,0:T(8,128)(2,1)}, bf16[16,512,128]{2,1,0:T(8,128)(2,1)}, f32[16,32]{1,0:T(8,128)}, f32[16,16]{1,0:T(8,128)}, f32[256,32]{...) custom-call(bf16[16,512,128]{2,1,0:T(8,128)(2,1)S(1)} %get-tuple-element.20.act, ...), custom_call_target="tpu_custom_call" | custom-call | tf_op jit(solution)/shard_map/pallas_call | solution.py:548

commit v5 on v4

--- a/solution.py
+++ b/solution.py
@@ -30,7 +30,7 @@
 CHUNK = 16
 FARTHEST = sorted(
     [(y, z) for y in range(4) for z in range(8) if y + z],
-    key=lambda step: (-min(step[0], 4 - step[0]) - min(step[1], 8 - step[1]), step),
+    key=lambda step: (-2 * min(step[0], 4 - step[0]) - min(step[1], 8 - step[1]), step),
 )
 CORE_SCALE = 1.0 / math.sqrt(GROUPS * PLANES * MX * MY)
 MIX_SCALE = 1.0 / math.sqrt(GROUPS * PLANES * NX * NY)
@@ -50,10 +50,11 @@
     first = np.concatenate([np.concatenate([a, b], axis=1), np.concatenate([-b, a], axis=1)], axis=0)
     first = first.reshape(2 * MX, 2, PENCILS, 2, HALF).transpose(0, 3, 2, 1, 4).reshape(2 * MX, 2 * NX)
     pad = np.zeros((NY, FEATS - 2 * MY))
+    ones = pad + (np.arange(FEATS - 2 * MY) < 3)
     pieces = (
         [second[FEATS * i : FEATS * (i + 1)].T for i in range(NY // FEATS)]
         + [first[:, FEATS * i : FEATS * (i + 1)] for i in range(2 * NX // FEATS)]
-        + [np.concatenate([second, pad], axis=1)]
+        + [np.concatenate([second, ones], axis=1)]
         + [np.concatenate([first.T, np.concatenate([pad, pad])], axis=1)]
     )
     return np.concatenate(pieces, axis=0).astype(np.float32).astype(jnp.bfloat16)
@@ -85,7 +86,7 @@
     act, adjoint, grads_out, second_out,
     field, cot, up, scratch, analysed, sbuf, rbuf,
     first_core, second_core, output_core, input_core, mix, bias, second_t, first, second, first_t,
-    joined_wide, out_wide, in_wide, mix_wide, mix_wide_t, bias_wide, narrow2, zed, spectrum, products, rows_sum, fold_rank, fold_lanes, misc,
+    joined_wide, out_wide, in_wide, mix_wide, mix_wide_t, bias_rows, narrow2, zed, spectrum, products, rows_sum, fold_rank, fold_lanes, misc,
     rest, gsend, grecv, bsend, brecv, csend,
     load_sem, small_sem, ssem, rsem, gssem, grsem, bssem, brsem, cssem, crsem,
 ):
@@ -220,7 +221,14 @@
         mix_wide[...] = jnp.where(same, dot(mix_rows, to_lanes), 0.0).astype(BF16)
         mix_rows = dot_nt(to_rows, mix[...]).astype(BF16)
         mix_wide_t[...] = jnp.where(same, dot(mix_rows, to_lanes), 0.0).astype(BF16)
-        bias_wide[...] = dot(bias[...], to_lanes.astype(F32), HIGHEST)
+        wide_bias = dot(bias[...], to_lanes.astype(F32), HIGHEST)
+        rows64, _ = iotas((2 * MY, FEATS))
+        terms = jnp.zeros((2 * MY, FEATS), F32)
+        for i in range(3):
+            term = wide_bias.astype(BF16).astype(F32)
+            terms = jnp.where(rows64 == i, term, terms)
+            wide_bias = wide_bias - term
+        bias_rows[...] = terms.astype(BF16)
         for part in range(4):
             load(cot_hbm, cot, 4 + part, 4 * part).wait()
 
@@ -235,10 +243,10 @@
         scatter_modes(1, dot(zed[...], out_wide[...]))
 
     def activate(x, rows_x):
-        rhs = jnp.concatenate([mix_wide[...], rows_x], axis=0)
+        rhs = jnp.concatenate([mix_wide[...], rows_x, bias_rows[...]], axis=0)
         for y in range(0, NY, 128):
-            lhs = jnp.concatenate([field[x, y : y + 128], second[y : y + 128, : 2 * MY]], axis=1)
-            combined = dot(lhs, rhs) + bias_wide[...]
+            lhs = jnp.concatenate([field[x, y : y + 128], second[y : y + 128]], axis=1)
+            combined = dot(lhs, rhs)
             cumulative = 0.5 + 0.5 * lax.erf(combined * math.sqrt(0.5))
             density = jnp.exp2(combined * combined * (-0.5 * math.log2(math.e))) * (1.0 / math.sqrt(2.0 * math.pi))
             act[x, y : y + 128] = (combined * cumulative).astype(BF16)
@@ -500,7 +508,7 @@
             pltpu.VMEM((FEATS, FEATS), BF16),
             pltpu.VMEM((FEATS, FEATS), BF16),
             pltpu.VMEM((FEATS, FEATS), BF16),
-            pltpu.VMEM((1, FEATS), F32),
+            pltpu.VMEM((2 * MY, FEATS), BF16),
             pltpu.VMEM((2 * MX, FEATS), F32),
             pltpu.VMEM((2 * MX, 1024), BF16),
             pltpu.VMEM((2 * MX, FEATS), F32),

time: 55.4 us -> 55.2 us (level)
  no operation moved by 1% of the time
where the time goes in v5:
time: 55.2 us; the launch traced here: 55 us
  Pallas kernels  54.4 us (99%)
  between operations  0.64 us (1%)
    pallas_call x1, Pallas kernels, shards(): pl.pallas_call(kernel, out_shape=[jax.ShapeDtypeStruct(slab, BF16), jax.S...  52.2 us
    pallas_call x1, Pallas kernels, shards(): pl.pallas_call(write_out, out_shape=[jax.ShapeDtypeStruct(slab, BF16), ja...  2.19 us

profile of v5, /device:TPU:1, one launch (start us, length us, event | category | flops | bytes accessed | tf_op | source)
XLA Modules:
  0.0 55.0 jit_solution(16045052297451099663)
XLA Ops:
  0.6 52.2 %shard_map.152 = (bf16[16,512,128]{2,1,0:T(8,128)(2,1)S(1)}, bf16[16,512,128]{2,1,0:T(8,128)(2,1)S(1)}, f32[8,16,128]{2,1,0:T(8,128)S(1)}, f32[16,128]{1,0:T(8,128)S(1)}) custom-call(bf16[16,512,128]{2,1,0:T(8,128)(2,1)} %bitcast.18, bf16[16,512,128]{2,1,0:T(8,128)(2,1)} %bitcast.19, f32[16,32]{1,0:T(8,128)} %bitcast.21, f32[16,16]{1,0:T(8,128)} %bitcast.22, ...), custom_call_target="tpu_custom_call" | custom-call | tf_op jit(solution)/shard_map/pallas_call | solution.py:481
  52.8 2.2 %shard_map.153 = (bf16[16,512,128]{2,1,0:T(8,128)(2,1)}, bf16[16,512,128]{2,1,0:T(8,128)(2,1)}, f32[16,32]{1,0:T(8,128)}, f32[16,16]{1,0:T(8,128)}, f32[256,32]{...) custom-call(bf16[16,512,128]{2,1,0:T(8,128)(2,1)S(1)} %get-tuple-element.20.act, ...), custom_call_target="tpu_custom_call" | custom-call | tf_op jit(solution)/shard_map/pallas_call | solution.py:556
